TPU v7x, 512 devices: a whole 4x8x8 slice. The times are simulated.
512 devices in a mesh: region: 32 (over y, z_hi), member: 16 (over x, z_lo, core).
Axes of the slice: x: 4, y: 8, z: 8 (z_hi: 4, z_lo: 2; z = z_hi * 2 + z_lo), core: 2. Of those that a mesh axis runs over, the one named last changes fastest.
Arguments:
- ensemble: bfloat16 [256, 262144], P('member', 'region'), may hold values from -6 to 6
- reports: float32 [32, 1024], P('region'), may hold values from -6 to 6
- report_count: int32 [32], P('region'), may hold values from 128 to 1024, as said below
- report_cell: int32 [32, 1024], P('region'), may hold values from 0 to 262143, as said below
- report_weight: float32 [32, 64, 1024], P('region', 'member'), may hold values from 0.001 to 1
- blending: float32 [4, 262144], P(None, ('region', 'member')), may hold values from 0.02 to 1
Outputs:
- analysis: bfloat16 [262144, 256], P(('region', 'member'))
Inputs may be any that keep to these rules, and one draw needn't show every extreme that they name: `report_count`: the largest value 1024 is reached by some region in every draw. `report_cell`: every cell lies in the slot's own region, or in the first 128 cells of one of at most two other regions chosen for that region.
All inputs are finite; a program needn't handle non-finite values.
Results may differ from a plain program's by a relative error of at most 0.0055.
Values may be sent and summed in bfloat16 or wider, within the bound.
A program may use at most 64 MiB of HBM per device.

v0:
```python
import jax
import jax.numpy as jnp
from jax import lax
from jax.sharding import PartitionSpec as P

MARGIN = 128
SWEEPS = 4


highest = lax.Precision.HIGHEST


def extended(block, sides, width):
    for axis, dim in sides:
        count = lax.axis_size(axis)
        forward = [(i, i + 1) for i in range(count - 1)]
        backward = [(target, source) for source, target in forward]
        low = lax.ppermute(
            lax.slice_in_dim(block, block.shape[dim] - width, None, axis=dim), axis, forward
        )
        high = lax.ppermute(lax.slice_in_dim(block, 0, width, axis=dim), axis, backward)
        block = jnp.concatenate([low, block, high], axis=dim)
    return block


def shifted(block, axis, distance):
    devices = range(lax.axis_size(axis))
    route = [(i - distance, i) for i in devices if i - distance in devices]
    return lax.ppermute(block, axis, route)


def make_transform(products, forcing, members):
    identity = jnp.eye(members, dtype=jnp.float32)
    precision_mat = (members - 1.0) * identity[None] + products
    frobenius = jnp.sqrt(jnp.sum(precision_mat * precision_mat, axis=(1, 2)))
    current = precision_mat / frobenius[:, None, None]
    root_iter = jnp.broadcast_to(identity, current.shape)
    for iteration in range(SWEEPS):
        middle = 1.5 * identity[None] - 0.5 * jnp.einsum(
            "aij,ajk->aik", root_iter, current, precision=highest
        )
        current = jnp.einsum("aij,ajk->aik", current, middle, precision=highest)
        root_iter = jnp.einsum("aij,ajk->aik", middle, root_iter, precision=highest)
    inverse_root = root_iter / jnp.sqrt(frobenius)[:, None, None]
    inner_step = jnp.einsum("aij,aj->ai", inverse_root, forcing, precision=highest)
    mean_weights = jnp.einsum("aij,aj->ai", inverse_root, inner_step, precision=highest)
    return (mean_weights[:, :, None] + jnp.sqrt(members - 1.0) * inverse_root).astype(jnp.bfloat16)


def corner_layout(band_index, points_here, row_count):
    group_index = jnp.arange(4 * points_here, dtype=jnp.int32)
    upper_half = group_index // (2 * points_here)
    column_block = group_index // 2 % points_here
    right_half = group_index % 2
    row_base = jnp.clip(band_index - 1 + upper_half, 0, row_count - 2)
    col_base = jnp.clip(column_block - 1 + right_half, 0, points_here - 2)
    return (row_base, col_base)


def per_device(ensemble, reports, report_count, report_cell, report_weight, blending):
    local_members, cell_count = ensemble.shape
    groups = lax.axis_size("member")
    members = local_members * groups
    region = lax.axis_index("region")
    member = lax.axis_index("member")
    targets = report_cell[0]
    holder = targets // cell_count
    within = targets % cell_count
    is_local = holder == region
    local_values = jnp.take(ensemble, jnp.where(is_local, within, 0), axis=1).astype(jnp.float32)
    border = ensemble[:, :MARGIN]
    border_index = holder * MARGIN + jnp.minimum(within, MARGIN - 1)
    pieces = lax.all_gather(border, "region", axis=1, tiled=True)
    extent = pieces.shape[1]
    inside = (border_index >= 0) & (border_index < extent) & jnp.logical_not(is_local)
    picked = jnp.take(pieces, jnp.clip(border_index, 0, extent - 1), axis=1).astype(jnp.float32)
    remote = jnp.where(inside[None, :], picked, 0.0)
    at_reports = jnp.where(is_local[None, :], local_values, remote)
    report_mean = lax.psum(jnp.sum(at_reports, axis=0), "member") / members
    local_pert = (at_reports - report_mean[None, :]).astype(jnp.bfloat16)
    report_pert = lax.all_gather(local_pert, "member", axis=0, tiled=True)
    active = (jnp.arange(report_pert.shape[1]) < report_count[0]).astype(jnp.float32)
    weights = report_weight[0] * active[None, :]
    weighted = (report_pert[None, :, :] * weights[:, None, :]).astype(jnp.bfloat16)
    departure = (weights * (reports[0] - report_mean)[None, :]).astype(jnp.bfloat16)
    products = jnp.einsum("ako,jo->akj", weighted, report_pert, preferred_element_type=jnp.float32)
    forcing = jnp.einsum("ao,ko->ak", departure, report_pert, preferred_element_type=jnp.float32)
    transform = make_transform(products, forcing, members)
    points_here = transform.shape[0]
    groups_band = 4 * points_here
    slab_cells = cell_count // groups
    group_cells = slab_cells // groups_band
    mixing = blending / jnp.sum(blending, axis=0, keepdims=True)
    everyone = lax.all_gather(ensemble, "member", axis=0, tiled=True)
    region_mean = jnp.sum(everyone, axis=0, dtype=jnp.float32) / members
    anomaly = (everyone - region_mean[None, :]).astype(jnp.bfloat16)
    near_mix = extended(mixing, (("member", 1),), slab_cells)
    totals = []
    for offset_band in range(3):
        band_index = member - 1 + offset_band
        slab_start = jnp.clip(band_index, 0, groups - 1) * slab_cells
        slab_anomaly = lax.dynamic_slice_in_dim(anomaly, slab_start, slab_cells, 1)
        slab_anomaly = slab_anomaly.reshape(members, groups_band, group_cells)
        mix_part = near_mix[:, offset_band * slab_cells : (offset_band + 1) * slab_cells]
        mix_part = mix_part.reshape(4, groups_band, group_cells)
        row_base, col_base = corner_layout(band_index, points_here, groups)
        row_step = (member - row_base)[:, None]
        running = jnp.zeros((groups_band, group_cells, members), jnp.float32)
        for col_step in range(2):
            weight = jnp.where(
                row_step == 0,
                mix_part[col_step],
                jnp.where(row_step == 1, mix_part[2 + col_step], 0.0),
            )
            chosen = jnp.take(transform, col_base + col_step, axis=0)
            spread = jnp.einsum(
                "kgc,gkj->gcj", slab_anomaly, chosen, preferred_element_type=jnp.float32
            )
            running = running + weight[:, :, None] * spread
        totals.append(running.reshape(slab_cells, members))
    from_below = shifted(totals[2], "member", 1)
    from_above = shifted(totals[0].astype(jnp.bfloat16), "member", -1).astype(jnp.float32)
    blended = totals[1] + from_below + from_above
    cell_mean = lax.dynamic_slice_in_dim(region_mean, member * slab_cells, slab_cells, 0)
    return (cell_mean[:, None] + blended).astype(jnp.bfloat16)


def solution(mesh):
    return jax.shard_map(
        per_device,
        mesh=mesh,
        in_specs=(
            P("member", "region"),
            P("region", None),
            P("region"),
            P("region", None),
            P("region", "member", None),
            P(None, ("region", "member")),
        ),
        out_specs=P(("region", "member"), None),
        check_vma=False,
    )
```

profile of v0, /device:TPU:1, one launch (start us, length us, event | category | flops | bytes accessed | tf_op | source)
XLA Modules:
  0.0 213.5 jit_solution(11608834173221068432)
XLA Ops:
  8.0 8.8 %collective-permute-start = (f32[4,512]{1,0:T(4,128)S(1)}, f32[4,512]{1,0:T(4,128)S(1)}, u32[]{:S(2)}, u32[]{:S(2)}) collective-permute-start(f32[4,512]{1,0:T(4,128)S(1)} %broadcast_divide_fusion.3), channel_id=1, source_target_pairs={{1,0},{2,1},{3,2},{4,3},{5,4},{6,5},{7,6},{8,7},{9,8},{10,9},{11,1... | collective-permute-start | bytes 24584 | tf_op jit(solution)/shard_map/ppermute | solution.py:21
  16.8 1.9 collective-permute-start.2
  18.7 1.9 copy.15
  20.8 3.2 %gather_fusion = bf16[1024,16]{1,0:T(8,128)(2,1)S(1)} fusion(bf16[16,8192]{0,1:T(8,128)(2,1)S(1)} %copy.15, s32[1024]{0:T(1024)S(1)} %broadcast_clamp_fusion.1), kind=kCustom, calls=%fused_computation.2 | custom fusion | bytes 69632 | tf_op jit(solution)/shard_map/jit(_take)/gather | solution.py:70
  24.1 76.4 %all_gather.10 = bf16[16,4096]{0,1:T(8,128)(2,1)S(1)} all-gather(bf16[16,128]{0,1:T(8,128)(2,1)S(1)} %slice.74), channel_id=1, replica_groups=mesh['region'=32,'member'=16] {'region'}, dimensions={1}, use_global_device_ids=true | all-gather | bytes 135168 | tf_op jit(solution)/shard_map/all_gather | solution.py:73
  100.5 3.2 %gather_fusion.1 = bf16[1024,16]{1,0:T(8,128)(2,1)S(1)} fusion(bf16[16,4096]{0,1:T(8,128)(2,1)S(1)} %all_gather.10, s32[1024]{0:T(1024)S(1)} %broadcast_clamp_fusion), kind=kCustom, calls=%fused_computation.3 | custom fusion | bytes 69632 | tf_op jit(solution)/shard_map/jit(_take)/gather | solution.py:76
  103.9 41.0 %psum.7 = f32[1024]{0:T(1024)S(1)} all-reduce(f32[1024]{0:T(1024)S(1)} %fusion.21), channel_id=1, replica_groups=mesh['region'=32,'member'=16] {'member'}, use_global_device_ids=true, to_apply=%region_3.4 | all-reduce | flops 1024 | bytes 8192 | tf_op jit(solution)/shard_map/psum | solution.py:79
  145.6 19.1 %all_gather.11 = bf16[256,1024]{1,0:T(8,128)(2,1)S(1)} all-gather(bf16[16,1024]{1,0:T(8,128)(2,1)S(1)} %fusion.22), channel_id=1, replica_groups=mesh['region'=32,'member'=16] {'member'}, dimensions={0}, use_global_device_ids=true | all-gather | bytes 557056 | tf_op jit(solution)/shard_map/all_gather | solution.py:81
  165.2 0.9 multiply_reduce_fusion
  166.0 1.2 fusion.8
  167.2 1.1 fusion.14
  168.3 1.2 fusion.20
  169.5 1.2 fusion.7
  170.7 1.1 fusion.42
  171.9 1.1 fusion.43
  173.0 1.2 fusion.6
  174.2 1.1 fusion.44
  175.4 1.1 fusion.45
  176.5 1.4 fusion.5
  177.9 1.1 convolution_divide_fusion
  179.1 1.0 fusion.28
  180.0 1.0 fusion.26
  182.5 2.0 gather_fusion.2
  185.4 3.0 %convert_reduce_fusion = f32[8192]{0:T(1024)S(1)} fusion(bf16[256,8192]{1,0:T(8,128)(2,1)} %all-gather.2.cloned.1.call-done), kind=kLoop, calls=%fused_computation.5 | loop fusion | flops 4186112 | bytes 4227072 | tf_op jit(solution)/shard_map/reduce_sum | solution.py:95
  188.8 0.9 fusion
  190.6 1.1 copy-done.1
  191.6 1.3 multiply_add_fusion
  192.9 2.8 %collective-permute-start.1 = (f32[512,256]{1,0:T(8,128)}, f32[512,256]{1,0:T(8,128)S(1)}, u32[]{:S(2)}, u32[]{:S(2)}) collective-permute-start(f32[512,256]{1,0:T(8,128)} %bitcast.16), channel_id=1, source_target_pairs={{0,1},{1,2},{2,3},{3,4},{4,5},{5,6},{6,7},{7,8},{8,9},{9,10},{10,1... | collective-permute-start | bytes 1572872 | tf_op jit(solution)/shard_map/ppermute | solution.py:29
  196.6 1.1 copy-done.2
  198.2 1.9 collective-permute-start.3
  201.2 4.6 %collective-permute-done.3 = bf16[512,256]{1,0:T(8,128)(2,1)S(1)} collective-permute-done((bf16[512,256]{1,0:T(8,128)(2,1)S(1)}, bf16[512,256]{1,0:T(8,128)(2,1)S(1)}, u32[]{:S(2)}, u32[]{:S(2)}) %collective-permute-start.3) | collective-permute-done | bytes 262176 | tf_op jit(solution)/shard_map/ppermute | solution.py:29
  205.9 0.8 fusion.12
  (80 shorter events, 8.2 us)
Async XLA Ops:
  6.5 14.1 %copy-start.3 = (s32[1,1024]{1,0:T(1,128)S(1)}, s32[1,1024]{1,0:T(1,128)}, u32[]{:S(2)}) copy-start(s32[1,1024]{1,0:T(1,128)} %param.11) | copy-start | bytes 12292
  6.5 178.8 %all-gather.2.cloned.1.call-start = ((), (), s32[]{:S(2)}) async-start(), calls=%async_computation | async-start | bytes 4456448 | tf_op jit(solution)/shard_map/all_gather | solution.py:94
  8.0 176.6 %collective-permute-start = (f32[4,512]{1,0:T(4,128)S(1)}, f32[4,512]{1,0:T(4,128)S(1)}, u32[]{:S(2)}, u32[]{:S(2)}) collective-permute-start(f32[4,512]{1,0:T(4,128)S(1)} %broadcast_divide_fusion.3), channel_id=1, source_target_pairs={{1,0},{2,1},{3,2},{4,3},{5,4},{6,5},{7,6},{8,7},{9,8},{10,9},{11,1... | collective-permute-start | bytes 24584 | tf_op jit(solution)/shard_map/ppermute | solution.py:21
  16.8 168.1 %collective-permute-start.2 = (f32[4,512]{1,0:T(4,128)S(1)}, f32[4,512]{1,0:T(4,128)S(1)}, u32[]{:S(2)}, u32[]{:S(2)}) collective-permute-start(f32[4,512]{1,0:T(4,128)S(1)} %broadcast_divide_fusion.3), channel_id=1, source_target_pairs={{0,1},{1,2},{2,3},{3,4},{4,5},{5,6},{6,7},{7,8},{8,9},{9,10},{10,1... | collective-permute-start | bytes 24584 | tf_op jit(solution)/shard_map/ppermute | solution.py:18
  18.7 126.2 %copy-start.5 = (f32[1,1024]{1,0:T(1,128)S(1)}, f32[1,1024]{1,0:T(1,128)}, u32[]{:S(2)}) copy-start(f32[1,1024]{1,0:T(1,128)} %param.9) | copy-start | bytes 12292
  100.5 64.4 %copy-start.4 = (f32[1,4,1024]{2,1,0:T(4,128)S(1)}, f32[1,4,1024]{2,1,0:T(4,128)}, u32[]{:S(2)}) copy-start(f32[1,4,1024]{2,1,0:T(4,128)} %param.12) | copy-start | bytes 49156
  185.4 3.5 %copy-start = (bf16[256,8192]{1,0:T(8,128)(2,1)S(1)}, bf16[256,8192]{1,0:T(8,128)(2,1)}, u32[]{:S(2)}) copy-start(bf16[256,8192]{1,0:T(8,128)(2,1)} %all-gather.2.cloned.1.call-done) | copy-start | bytes 12582916
  190.0 1.6 copy-start.1
  192.9 12.9 %collective-permute-start.1 = (f32[512,256]{1,0:T(8,128)}, f32[512,256]{1,0:T(8,128)S(1)}, u32[]{:S(2)}, u32[]{:S(2)}) collective-permute-start(f32[512,256]{1,0:T(8,128)} %bitcast.16), channel_id=1, source_target_pairs={{0,1},{1,2},{2,3},{3,4},{4,5},{5,6},{6,7},{7,8},{8,9},{9,10},{10,1... | collective-permute-start | bytes 1572872 | tf_op jit(solution)/shard_map/ppermute | solution.py:29
  196.0 1.6 copy-start.2
  198.2 7.7 %collective-permute-start.3 = (bf16[512,256]{1,0:T(8,128)(2,1)S(1)}, bf16[512,256]{1,0:T(8,128)(2,1)S(1)}, u32[]{:S(2)}, u32[]{:S(2)}) collective-permute-start(bf16[512,256]{1,0:T(8,128)(2,1)S(1)} %bitcast.89), channel_id=1, source_target_pairs={{1,0},{2,1},{3,2},{4,3},{5,4},{6,5},{7,6},{8,7},{9,8},{10,9},{11,1... | collective-permute-start | bytes 786440 | tf_op jit(solution)/shard_map/ppermute | solution.py:29
Sparse Core Ops, SparseCore 0:
  18.8 47.7 all-gather.1
where the time goes:
time: 214 us
  blocking collectives  136 us (64%)
  matrix products  19.9 us (9%)
  local copies, waits for them, and re-layouts  15.4 us (7%)
  starting transfers between devices  15.4 us (7%)
  between operations  14.5 us (7%)
  other arithmetic  7.2 us (3%)
  waiting for transfers between devices  4.65 us (2%)
    all_gather x1, blocking collectives, per_device(): pieces = lax.all_gather(border, 'region', axis=1, tiled=True)  76.4 us
    psum x1, blocking collectives, per_device(): report_mean = lax.psum(jnp.sum(at_reports, axis=0), 'member') / members  41 us
    all_gather x1, blocking collectives, per_device(): report_pert = lax.all_gather(local_pert, 'member', axis=0, tiled=True)  19.1 us
    ppermute x1, starting transfers between devices, extended(): lax.ppermute(lax.slice_in_dim(block, 0, width, axis=dim), axis, backward)  8.78 us
    dot_general x4, matrix products, make_transform(): jnp.einsum('aij,ajk->aik', root_iter, current, precision=highest)  4.9 us
    ppermute x2, starting transfers between devices, shifted(): return lax.ppermute(block, axis, route)  4.74 us
    ppermute x2, waiting for transfers between devices, shifted(): return lax.ppermute(block, axis, route)  4.63 us
    dot_general x4, matrix products, make_transform(): root_iter = jnp.einsum('aij,ajk->aik', middle, root_iter, precision=highest)  4.53 us
  transfers between devices with their start and end apart: 5, of which 1 were waited for; matrix products, arithmetic and copies ran while one was open for 15% of the time, Pallas kernels for 0%

commit v1 on v0

v1 whole, which is shorter than its diff:
```python
import functools
import math

import jax
import jax.numpy as jnp
from jax import lax
from jax.experimental import pallas as pl
from jax.experimental.pallas import tpu as pltpu
from jax.sharding import PartitionSpec as P

MESH = pl.DeviceIdType.MESH
MARGIN = 128
F32 = jnp.float32
BF16 = jnp.bfloat16


def split(value):
    high = value.astype(BF16)
    low = (value - high.astype(F32)).astype(BF16)
    return high, low


def dot(a, b):
    return jnp.dot(a, b, preferred_element_type=F32)


def dot_nt(a, b):
    return lax.dot_general(a, b, (((1,), (1,)), ((), ())), preferred_element_type=F32)


def left(parts):
    high, low = parts
    return jnp.concatenate([high, high, low], axis=1)


def right(parts):
    high, low = parts
    return jnp.concatenate([high, low, high], axis=0)


def kernel(
    count_ref, ens_ref, rep_ref, cell_ref, rw_ref, bl_ref, out_ref,
    at_buf, cells_buf, extra_buf, bl_buf, bord, fwd, picked, sent, got, anom, extra_anom, mean_col,
    x_s, z_s, t_s, forcing_s,
    bz_send, bz_recv, by_send, by_recv, at_send, at_recv, ce_send, ce_recv, fw_send, fw_recv,
    bl_send, bl_recv, xs_send, xs_recv, cn_send, cn_recv,
):
    region = lax.axis_index("region")
    me = lax.axis_index("member")
    local, cells = ens_ref.shape
    n = 16
    members = n * local
    zs, ys = 4, 8
    y, z = region // zs, region % zs
    half = cells // n // 2
    slots = at_buf.shape[1]
    first = (n - 1 - me) // (n - 1)
    last = me // (n - 1)

    def peer(i):
        return lax.rem(me + i, n)

    def zpeer(i):
        return y * zs + lax.rem(z + i, zs)

    def ypeer(i):
        return lax.rem(y + i, ys) * zs + z

    def rows(d):
        return pl.ds(pl.multiple_of(d * local, local), local)

    def remote(src, dst, ss, rs, **where):
        return pltpu.make_async_remote_copy(
            src_ref=src, dst_ref=dst, send_sem=ss, recv_sem=rs, device_id=where, device_id_type=MESH
        )

    barrier = pltpu.get_barrier_semaphore()

    def greet(i, c):
        pl.semaphore_signal(barrier, inc=1, device_id={"member": peer(i)}, device_id_type=MESH)
        return c

    def greet_z(i, c):
        pl.semaphore_signal(barrier, inc=1, device_id={"region": zpeer(i)}, device_id_type=MESH)
        return c

    def greet_y(i, c):
        pl.semaphore_signal(barrier, inc=1, device_id={"region": ypeer(i)}, device_id_type=MESH)
        return c

    lax.fori_loop(1, zs, greet_z, 0)
    lax.fori_loop(1, ys, greet_y, 0)
    lax.fori_loop(1, n, greet, 0)
    pl.semaphore_wait(barrier, zs + ys + n - 3)

    def z_copy(i):
        return remote(ens_ref.at[:, pl.ds(0, MARGIN)], bord.at[region], bz_send.at[i], bz_recv.at[i], region=zpeer(i))

    def y_copy(i):
        block = bord.at[pl.ds(y * zs, zs)]
        return remote(block, block, by_send.at[i], by_recv.at[i], region=ypeer(i))

    def at_copy(i):
        block = at_buf.at[rows(me)]
        return remote(block, block, at_send.at[i], at_recv.at[i], member=peer(i))

    def cell_start(d):
        return pl.multiple_of(2 * half * d - half + half * ((n - 1 - d) // (n - 1)) - half * (d // (n - 1)), MARGIN)

    def ce_copy(i):
        source = ens_ref.at[:, pl.ds(cell_start(peer(i)), 4 * half)]
        return remote(source, cells_buf.at[rows(me)], ce_send.at[i], ce_recv.at[i], member=peer(i))

    def fw_copy(i):
        return remote(fwd, picked.at[rows(me)], fw_send.at[i], fw_recv.at[i], member=peer(i))

    def started(copy):
        def body(i, c):
            copy(i).start()
            return c
        return body

    def sent_off(copy):
        def body(i, c):
            copy(i).wait_send()
            return c
        return body

    def arrived(copy):
        def body(i, c):
            copy(i).wait_recv()
            return c
        return body

    lax.fori_loop(1, zs, started(z_copy), 0)
    bord[region] = ens_ref[:, pl.ds(0, MARGIN)]

    up = remote(bl_ref, bl_buf.at[0], bl_send.at[0], bl_recv.at[0], member=lax.rem(me + 1, n))
    down = remote(bl_ref, bl_buf.at[1], bl_send.at[1], bl_recv.at[1], member=lax.rem(me + n - 1, n))
    up.start()
    down.start()

    lax.fori_loop(1, zs, arrived(z_copy), 0)
    lax.fori_loop(1, ys, started(y_copy), 0)

    target = cell_ref[...]
    relative = target - region * cells
    is_local = (relative >= 0) & (relative < cells)
    lane = lax.rem(jnp.where(is_local, relative, 0), MARGIN)
    column = jnp.where(is_local, relative // MARGIN, -1)
    blocks = slots // MARGIN
    lanes = [jnp.broadcast_to(lane[:, b * MARGIN:(b + 1) * MARGIN], (local, MARGIN)) for b in range(blocks)]
    columns = [jnp.broadcast_to(column[:, b * MARGIN:(b + 1) * MARGIN], (local, MARGIN)) for b in range(blocks)]

    def gather(h, accs):
        chunk = ens_ref[:, pl.ds(pl.multiple_of(h * MARGIN, MARGIN), MARGIN)].astype(F32)
        return tuple(
            jnp.where(columns[b] == h, jnp.take_along_axis(chunk, lanes[b], axis=1, mode="promise_in_bounds"), accs[b])
            for b in range(blocks)
        )

    accs = lax.fori_loop(0, cells // MARGIN, gather, tuple(jnp.zeros((local, MARGIN), F32) for _ in range(blocks)))
    at_buf[rows(me), :] = jnp.concatenate(accs, axis=1).astype(BF16)
    lax.fori_loop(1, n, started(at_copy), 0)

    holder = (target // cells).astype(F32)
    s_low = jnp.min(jnp.where(is_local, 1e6, holder), axis=1, keepdims=True)
    s_high = jnp.max(jnp.where(is_local, -1.0, holder), axis=1, keepdims=True)
    lax.fori_loop(1, ys, arrived(y_copy), 0)

    def pick(s, c):
        low, high = c
        block = bord[s].astype(F32)
        at = s.astype(F32)
        return jnp.where(s_low == at, block, low), jnp.where(s_high == at, block, high)

    nothing = jnp.zeros((local, MARGIN), F32)
    low, high = lax.fori_loop(0, zs * ys, pick, (nothing, nothing))
    mine = jnp.concatenate([low, high], axis=1).astype(BF16)
    fwd[...] = mine
    picked[rows(me), :] = mine
    lax.fori_loop(1, n, started(fw_copy), 0)

    lax.fori_loop(1, n, started(ce_copy), 0)
    cells_buf[rows(me), :] = ens_ref[:, pl.ds(cell_start(me), 4 * half)]

    def extra_copy(k):
        d = (1, n - 2)[k]
        source = ens_ref.at[:, pl.ds((0, cells - half)[k], half)]
        return remote(source, extra_buf.at[rows(me)], xs_send.at[k], xs_recv.at[me], member=d)

    for k, d in enumerate((1, n - 2)):
        @pl.when(me != d)
        def _():
            extra_copy(k).start()

        @pl.when(me == d)
        def _():
            extra_buf[rows(me), :] = ens_ref[:, pl.ds((0, cells - half)[k], half)]

    lax.fori_loop(1, n, arrived(fw_copy), 0)
    lax.fori_loop(1, n, arrived(at_copy), 0)
    within = lax.rem(target, cells)
    key = jnp.where(
        is_local, -1,
        jnp.where(holder == s_low, within, jnp.where(holder == s_high, MARGIN + within, -1)),
    )
    onehot = (lax.broadcasted_iota(jnp.int32, (2 * MARGIN, slots), 0) == key).astype(F32).astype(BF16)
    at_reports = at_buf[...].astype(F32) + dot(picked[...], onehot)
    mean = jnp.sum(at_reports, axis=0, keepdims=True) * (1.0 / members)
    pert = (at_reports - mean).astype(BF16)
    pert_wide = pert.astype(F32)
    active = lax.broadcasted_iota(jnp.int32, (1, slots), 1) < count_ref[0]
    weights = jnp.where(active, rw_ref[...], 0.0)
    points = weights.shape[0]
    departure = weights * (rep_ref[...] - mean)
    departure = jnp.concatenate([departure, jnp.zeros((MARGIN - points, slots), F32)], axis=0).astype(BF16)
    forcing_s[...] = dot_nt(pert, departure)
    eye = (
        lax.broadcasted_iota(jnp.int32, (members, members), 0)
        == lax.broadcasted_iota(jnp.int32, (members, members), 1)
    ).astype(F32)
    frob = []
    for q in range(points):
        weighted = (pert_wide * weights[q:q + 1]).astype(BF16)
        precision_mat = (members - 1.0) * eye + dot_nt(weighted, pert)
        squares = jnp.sum(jnp.sum(precision_mat * precision_mat, axis=0, keepdims=True), axis=1, keepdims=True)
        f = jnp.sqrt(squares)
        frob.append(f)
        a = precision_mat * (1.0 / f)
        middle = 1.5 * eye - 0.5 * a
        m = right(split(middle))
        inner = dot(left(split(a)), m)
        x_s[q] = dot(left(split(inner)), m)
        z_s[q] = middle

    def sweep(i, c):
        for q in range(points):
            x = x_s[q]
            m = right(split(1.5 * eye - 0.5 * x))
            inner = dot(left(split(x)), m)
            z_s[q] = dot(left(split(z_s[q])), m)
            x_s[q] = dot(left(split(inner)), m)
        return c

    lax.fori_loop(0, 2, sweep, 0)
    for q in range(points):
        m = right(split(1.5 * eye - 0.5 * x_s[q]))
        root = dot(left(split(z_s[q])), m)
        root_parts = left(split(root))
        step = dot(root_parts, right(split(forcing_s[...])))
        mean_weights = dot(root_parts, right(split(step))) * (1.0 / frob[q])
        t_s[q] = (mean_weights[:, q:q + 1] + (math.sqrt(members - 1.0) * lax.rsqrt(frob[q])) * root).astype(BF16)

    lax.fori_loop(1, n, arrived(ce_copy), 0)

    def turn(values):
        across = values.astype(F32).T
        mean = jnp.sum(across, axis=1, keepdims=True) * (1.0 / members)
        return mean, (across - mean).astype(BF16)

    for b in range(4):
        cut = slice(b * half, (b + 1) * half)
        mean_col[cut], anom[cut] = turn(cells_buf[:, cut])

    up.wait_recv()
    down.wait_recv()

    def mixed(values):
        return values * (1.0 / jnp.sum(values, axis=0, keepdims=True))

    own, below, above = mixed(bl_ref[...]), mixed(bl_buf[0]), mixed(bl_buf[1])
    weights_of = [
        below[2:4, half:],
        jnp.where(me == 0, own[0:2, :half], own[2:4, :half]),
        jnp.where(me == n - 1, own[2:4, half:], own[0:2, half:]),
        above[0:2, :half],
        jnp.where(me == 1, below[2:4, :half], above[0:2, half:]),
    ]
    stacked = jnp.concatenate(weights_of + [jnp.zeros((MARGIN - 10, half), F32)], axis=0)
    mix = stacked.T

    narrow, wide = 3 * half // 8, 5 * half // 8

    def blended(values, b):
        w0, w1 = mix[:, 2 * b:2 * b + 1], mix[:, 2 * b + 1:2 * b + 2]
        s0 = dot(values[:narrow], t_s[0])
        s1 = dot(values[:wide], t_s[1])
        s2 = dot(values[narrow:], t_s[2])
        s3 = dot(values[wide:], t_s[3])
        return jnp.concatenate([
            w0[:narrow] * s0 + w1[:narrow] * s1[:narrow],
            w0[narrow:wide] * s1[narrow:] + w1[narrow:wide] * s2[:wide - narrow],
            w0[wide:] * s2[wide - narrow:] + w1[wide:] * s3,
        ], axis=0)

    base = pl.multiple_of(half * (1 - first + last), half)

    def part(offset):
        return pl.ds(pl.multiple_of(base + offset, half), half)

    def out_copy(k, d, side):
        return remote(sent.at[k], got.at[side], cn_send.at[k], cn_recv.at[side], member=d)

    @pl.when(me < n - 1)
    def _():
        sent[0] = blended(anom[part(2 * half)], 3).astype(BF16)
        out_copy(0, me + 1, 0).start()

    @pl.when(me > 0)
    def _():
        sent[1] = blended(anom[part(-half)], 0).astype(BF16)
        out_copy(1, me - 1, 1).start()

    for k, d, target_d, side in ((0, 1, 0, 0), (1, n - 2, n - 1, 1)):
        @pl.when(me == d)
        def _():
            def extra_in(i, c):
                src = peer(i)
                remote(
                    ens_ref.at[:, pl.ds(0, half)], extra_buf.at[rows(src)], xs_send.at[k], xs_recv.at[src], member=src
                ).wait_recv()
                return c

            lax.fori_loop(1, n, extra_in, 0)
            sent[2] = blended(turn(extra_buf[...])[1], 4).astype(BF16)
            out_copy(2, target_d, side).start()

    mine_0 = mean_col[part(0)] + blended(anom[part(0)], 1)
    mine_1 = mean_col[part(half)] + blended(anom[part(half)], 2)
    out_copy(0, lax.rem(me + 1, n), 0).wait_recv()
    out_ref[:half] = (mine_0 + got[0].astype(F32)).astype(BF16)
    out_copy(1, lax.rem(me + n - 1, n), 1).wait_recv()
    out_ref[half:] = (mine_1 + got[1].astype(F32)).astype(BF16)

    lax.fori_loop(1, zs, sent_off(z_copy), 0)
    lax.fori_loop(1, ys, sent_off(y_copy), 0)
    lax.fori_loop(1, n, sent_off(at_copy), 0)
    lax.fori_loop(1, n, sent_off(fw_copy), 0)
    lax.fori_loop(1, n, sent_off(ce_copy), 0)
    up.wait_send()
    down.wait_send()
    for k, d in enumerate((1, n - 2)):
        @pl.when(me != d)
        def _():
            extra_copy(k).wait_send()

        @pl.when(me == d)
        def _():
            out_copy(2, 0, 0).wait_send()

    @pl.when(me < n - 1)
    def _():
        out_copy(0, me + 1, 0).wait_send()

    @pl.when(me > 0)
    def _():
        out_copy(1, me - 1, 1).wait_send()


def per_device(ensemble, reports, report_count, report_cell, report_weight, blending):
    local, cells = ensemble.shape
    n = lax.axis_size("member")
    members = n * local
    slots = reports.shape[1]
    points = report_weight.shape[1]
    half = cells // n // 2
    vmem = pl.BlockSpec(memory_space=pltpu.VMEM)
    dma = pltpu.SemaphoreType.DMA
    return pl.pallas_call(
        kernel,
        out_shape=jax.ShapeDtypeStruct((cells // n, members), BF16),
        in_specs=[pl.BlockSpec(memory_space=pltpu.SMEM)] + [vmem] * 5,
        out_specs=vmem,
        scratch_shapes=[
            pltpu.VMEM((members, slots), BF16),
            pltpu.VMEM((members, 4 * half), BF16),
            pltpu.VMEM((members, half), BF16),
            pltpu.VMEM((2, 4, 2 * half), F32),
            pltpu.VMEM((lax.axis_size("region"), local, MARGIN), BF16),
            pltpu.VMEM((local, 2 * MARGIN), BF16),
            pltpu.VMEM((members, 2 * MARGIN), BF16),
            pltpu.VMEM((3, half, members), BF16),
            pltpu.VMEM((2, half, members), BF16),
            pltpu.VMEM((4 * half, members), BF16),
            pltpu.VMEM((half, members), BF16),
            pltpu.VMEM((4 * half, 1), F32),
            pltpu.VMEM((points, members, members), F32),
            pltpu.VMEM((points, members, members), F32),
            pltpu.VMEM((points, members, members), BF16),
            pltpu.VMEM((members, MARGIN), F32),
            dma((4,)), dma((4,)), dma((8,)), dma((8,)), dma((n,)), dma((n,)), dma((n,)), dma((n,)), dma((n,)), dma((n,)),
            dma((2,)), dma((2,)), dma((2,)), dma((n,)), dma((3,)), dma((2,)),
        ],
        compiler_params=pltpu.CompilerParams(
            collective_id=0, has_side_effects=True, vmem_limit_bytes=48 * 1024 * 1024
        ),
    )(report_count, ensemble, reports, report_cell, report_weight[0], blending)


def solution(mesh):
    return jax.shard_map(
        per_device,
        mesh=mesh,
        in_specs=(
            P("member", "region"),
            P("region", None),
            P("region"),
            P("region", None),
            P("region", "member", None),
            P(None, ("region", "member")),
        ),
        out_specs=P(("region", "member"), None),
        check_vma=False,
    )
```

time: 214 us -> 58.7 us (0.27)
  blocking collectives: 136 us -> 0 us
  Pallas kernels: 0 us -> 53.3 us
  matrix products: 19.9 us -> 0 us
  starting transfers between devices: 15.4 us -> 0 us
  between operations: 14.5 us -> 0.67 us
  local copies, waits for them, and re-layouts: 15.4 us -> 4.43 us
  other arithmetic: 7.2 us -> 0 us
  waiting for transfers between devices: 4.65 us -> 0 us
    all_gather x2 -> x0, blocking collectives: 95.4 us -> none  [the longest x1 76.4 us: per_device(): pieces = lax.all_gather(border, 'region', axis=1, tiled=True)]
    pallas_call x0 -> x1, Pallas kernels: none -> 53.3 us  [per_device(): pl.pallas_call(kernel, out_shape=jax.ShapeDtypeStruct((cells // n, member...]
    psum x1 -> x0, blocking collectives: 41 us -> none  [per_device(): report_mean = lax.psum(jnp.sum(at_reports, axis=0), 'member') / members]
    dot_general x21 -> x0, matrix products: 19.9 us -> none  [the longest x4 4.9 us: make_transform(): jnp.einsum('aij,ajk->aik', root_iter, current, precision=highest)]
    ppermute x4 -> x0, starting transfers between devices: 15.4 us -> none  [the longest x1 8.78 us: extended(): lax.ppermute(lax.slice_in_dim(block, 0, width, axis=dim), axis, backward)]
    gather x6 -> x0, local copies, waits for them, and re-layouts: 9.32 us -> none  [the longest x2 3.32 us: per_device(): jnp.take(ensemble, jnp.where(is_local, within, 0), axis=1)]
    ppermute x4 -> x0, waiting for transfers between devices: 4.63 us -> none  [the longest x2 4.63 us: shifted(): return lax.ppermute(block, axis, route)]
    reduce_sum x3 -> x0, other arithmetic: 3.8 us -> none  [the longest x1 3.04 us: per_device(): region_mean = jnp.sum(everyone, axis=0, dtype=jnp.float32) / members]
  transfers between devices with their start and end apart: 5 -> 0, of which waited for: 1 -> 0; matrix products, arithmetic and copies ran while one was open for 15% -> 0% of each run, Pallas kernels for 0% -> 0%
where the time goes in v1:
time: 58.7 us; the launch traced here: 58.4 us
  Pallas kernels  53.3 us (91%)
  local copies, waits for them, and re-layouts  4.43 us (8%)
  between operations  0.67 us (1%)
    pallas_call x1, Pallas kernels, per_device(): pl.pallas_call(kernel, out_shape=jax.ShapeDtypeStruct((cells // n, member...  53.3 us
    unnamed x11, local copies, waits for them, and re-layouts  4.43 us

profile of v1, /device:TPU:1, one launch (start us, length us, event | category | flops | bytes accessed | tf_op | source)
XLA Modules:
  0.0 58.4 jit_solution(17662539669858584893)
XLA Ops:
  0.7 0.0 copy-start
  0.7 0.9 %copy-done = bf16[16,8192]{1,0:T(8,128)(2,1)S(1)} copy-done((bf16[16,8192]{1,0:T(8,128)(2,1)S(1)}, bf16[16,8192]{1,0:T(8,128)(2,1)}, u32[]{:S(2)}) %copy-start) | copy-done | bytes 262168
  1.6 0.0 copy-start.1
  1.6 0.7 %copy-done.1 = f32[1,4,1024]{2,1,0:T(4,128)S(1)} copy-done((f32[1,4,1024]{2,1,0:T(4,128)S(1)}, f32[1,4,1024]{2,1,0:T(4,128)}, u32[]{:S(2)}) %copy-start.1) | copy-done | bytes 16408
  2.3 0.0 copy-start.2
  2.3 0.7 %copy-done.2 = f32[4,512]{1,0:T(4,128)S(1)} copy-done((f32[4,512]{1,0:T(4,128)S(1)}, f32[4,512]{1,0:T(4,128)}, u32[]{:S(2)}) %copy-start.2) | copy-done | bytes 8216
  3.0 0.0 copy-start.3
  3.0 0.7 %copy-done.3 = f32[1,1024]{1,0:T(1,128)S(1)} copy-done((f32[1,1024]{1,0:T(1,128)S(1)}, f32[1,1024]{1,0:T(1,128)}, u32[]{:S(2)}) %copy-start.3) | copy-done | bytes 4120
  3.7 0.0 copy-start.4
  3.7 0.7 %copy-done.4 = s32[1,1024]{1,0:T(1,128)S(1)} copy-done((s32[1,1024]{1,0:T(1,128)S(1)}, s32[1,1024]{1,0:T(1,128)}, u32[]{:S(2)}) %copy-start.4) | copy-done | bytes 4120
  4.4 53.3 %shard_map.64 = bf16[512,256]{1,0:T(8,128)(2,1)S(1)} custom-call(s32[1]{0:T(128)S(6)} %copy.8.count_ref, bf16[16,8192]{1,0:T(8,128)(2,1)S(1)} %copy-done, f32[1,1024]{1,0:T(1,128)S(1)} %copy-done.3, s32[1,1024]{1,0:T(1,128)S(1)} %copy-done.4, f32[4,1024]{1,0:T(4,128)S(1)} %bitcast.1, f32[4,512]{1,0:T(4,128)S(1)} %copy-done.2), custom_call_target="tpu_custom_call" | custom-call | tf_op jit(solution)/shard_map/pallas_call | solution.py:370
  57.7 0.7 %copy.9 = bf16[512,256]{1,0:T(8,128)(2,1)} copy(bf16[512,256]{1,0:T(8,128)(2,1)S(1)} %shard_map.64) | data formatting | bytes 524288
Async XLA Ops:
  0.7 1.0 %copy-start = (bf16[16,8192]{1,0:T(8,128)(2,1)S(1)}, bf16[16,8192]{1,0:T(8,128)(2,1)}, u32[]{:S(2)}) copy-start(bf16[16,8192]{1,0:T(8,128)(2,1)} %ens_ref.1) | copy-start | bytes 786436
  1.6 0.7 %copy-start.1 = (f32[1,4,1024]{2,1,0:T(4,128)S(1)}, f32[1,4,1024]{2,1,0:T(4,128)}, u32[]{:S(2)}) copy-start(f32[1,4,1024]{2,1,0:T(4,128)} %param.10) | copy-start | bytes 49156
  2.3 0.7 %copy-start.2 = (f32[4,512]{1,0:T(4,128)S(1)}, f32[4,512]{1,0:T(4,128)}, u32[]{:S(2)}) copy-start(f32[4,512]{1,0:T(4,128)} %bl_ref.1) | copy-start | bytes 24580
  3.0 0.7 %copy-start.3 = (f32[1,1024]{1,0:T(1,128)S(1)}, f32[1,1024]{1,0:T(1,128)}, u32[]{:S(2)}) copy-start(f32[1,1024]{1,0:T(1,128)} %rep_ref.1) | copy-start | bytes 12292
  3.7 0.7 %copy-start.4 = (s32[1,1024]{1,0:T(1,128)S(1)}, s32[1,1024]{1,0:T(1,128)}, u32[]{:S(2)}) copy-start(s32[1,1024]{1,0:T(1,128)} %cell_ref.1) | copy-start | bytes 12292

commit v2 on v1

--- a/solution.py
+++ b/solution.py
@@ -28,6 +28,10 @@
     return lax.dot_general(a, b, (((1,), (1,)), ((), ())), preferred_element_type=F32)
 
 
+def dot_tn(a, b):
+    return lax.dot_general(a, b, (((0,), (0,)), ((), ())), preferred_element_type=F32)
+
+
 def left(parts):
     high, low = parts
     return jnp.concatenate([high, high, low], axis=1)
@@ -39,19 +43,27 @@
 
 
 def kernel(
-    count_ref, ens_ref, rep_ref, cell_ref, rw_ref, bl_ref, out_ref,
+    count_hbm, ens_hbm, rep_hbm, cell_hbm, rw_hbm, bl_hbm, out_ref,
+    count_ref, ens_ref, rep_ref, cell_ref, rw_ref, bl_ref, in_sem,
     at_buf, cells_buf, extra_buf, bl_buf, bord, fwd, picked, sent, got, anom, extra_anom, mean_col,
-    x_s, z_s, t_s, forcing_s,
-    bz_send, bz_recv, by_send, by_recv, at_send, at_recv, ce_send, ce_recv, fw_send, fw_recv,
+    wide_ens, x_s, z_s, t_s, forcing_s,
+    bo_send, bo_recv, at_send, at_recv, ce_send, ce_recv, fw_send, fw_recv,
     bl_send, bl_recv, xs_send, xs_recv, cn_send, cn_recv,
 ):
+    loads = [
+        pltpu.make_async_copy(source, landed, in_sem.at[i])
+        for i, (source, landed) in enumerate((
+            (cell_hbm, cell_ref), (ens_hbm, ens_ref), (bl_hbm, bl_ref), (rw_hbm, rw_ref), (rep_hbm, rep_ref), (count_hbm, count_ref)
+        ))
+    ]
+    for load in loads:
+        load.start()
     region = lax.axis_index("region")
     me = lax.axis_index("member")
     local, cells = ens_ref.shape
     n = 16
     members = n * local
-    zs, ys = 4, 8
-    y, z = region // zs, region % zs
+    regions = bord.shape[0]
     half = cells // n // 2
     slots = at_buf.shape[1]
     first = (n - 1 - me) // (n - 1)
@@ -60,11 +72,8 @@
     def peer(i):
         return lax.rem(me + i, n)
 
-    def zpeer(i):
-        return y * zs + lax.rem(z + i, zs)
-
-    def ypeer(i):
-        return lax.rem(y + i, ys) * zs + z
+    def region_peer(i):
+        return lax.rem(region + i, regions)
 
     def rows(d):
         return pl.ds(pl.multiple_of(d * local, local), local)
@@ -80,25 +89,18 @@
         pl.semaphore_signal(barrier, inc=1, device_id={"member": peer(i)}, device_id_type=MESH)
         return c
 
-    def greet_z(i, c):
-        pl.semaphore_signal(barrier, inc=1, device_id={"region": zpeer(i)}, device_id_type=MESH)
+    def greet_region(i, c):
+        pl.semaphore_signal(barrier, inc=1, device_id={"region": region_peer(i)}, device_id_type=MESH)
         return c
 
-    def greet_y(i, c):
-        pl.semaphore_signal(barrier, inc=1, device_id={"region": ypeer(i)}, device_id_type=MESH)
-        return c
-
-    lax.fori_loop(1, zs, greet_z, 0)
-    lax.fori_loop(1, ys, greet_y, 0)
+    lax.fori_loop(1, regions, greet_region, 0)
     lax.fori_loop(1, n, greet, 0)
-    pl.semaphore_wait(barrier, zs + ys + n - 3)
-
-    def z_copy(i):
-        return remote(ens_ref.at[:, pl.ds(0, MARGIN)], bord.at[region], bz_send.at[i], bz_recv.at[i], region=zpeer(i))
-
-    def y_copy(i):
-        block = bord.at[pl.ds(y * zs, zs)]
-        return remote(block, block, by_send.at[i], by_recv.at[i], region=ypeer(i))
+    for load in loads:
+        load.wait()
+
+    def border_copy(i):
+        source = ens_ref.at[:, pl.ds(0, MARGIN)]
+        return remote(source, bord.at[region], bo_send.at[i], bo_recv.at[i], region=region_peer(i))
 
     def at_copy(i):
         block = at_buf.at[rows(me)]
@@ -132,41 +134,35 @@
             return c
         return body
 
-    lax.fori_loop(1, zs, started(z_copy), 0)
-    bord[region] = ens_ref[:, pl.ds(0, MARGIN)]
-
-    up = remote(bl_ref, bl_buf.at[0], bl_send.at[0], bl_recv.at[0], member=lax.rem(me + 1, n))
-    down = remote(bl_ref, bl_buf.at[1], bl_send.at[1], bl_recv.at[1], member=lax.rem(me + n - 1, n))
-    up.start()
-    down.start()
-
-    lax.fori_loop(1, zs, arrived(z_copy), 0)
-    lax.fori_loop(1, ys, started(y_copy), 0)
-
     target = cell_ref[...]
     relative = target - region * cells
     is_local = (relative >= 0) & (relative < cells)
     lane = lax.rem(jnp.where(is_local, relative, 0), MARGIN)
     column = jnp.where(is_local, relative // MARGIN, -1)
-    blocks = slots // MARGIN
-    lanes = [jnp.broadcast_to(lane[:, b * MARGIN:(b + 1) * MARGIN], (local, MARGIN)) for b in range(blocks)]
-    columns = [jnp.broadcast_to(column[:, b * MARGIN:(b + 1) * MARGIN], (local, MARGIN)) for b in range(blocks)]
-
-    def gather(h, accs):
-        chunk = ens_ref[:, pl.ds(pl.multiple_of(h * MARGIN, MARGIN), MARGIN)].astype(F32)
-        return tuple(
-            jnp.where(columns[b] == h, jnp.take_along_axis(chunk, lanes[b], axis=1, mode="promise_in_bounds"), accs[b])
-            for b in range(blocks)
-        )
-
-    accs = lax.fori_loop(0, cells // MARGIN, gather, tuple(jnp.zeros((local, MARGIN), F32) for _ in range(blocks)))
-    at_buf[rows(me), :] = jnp.concatenate(accs, axis=1).astype(BF16)
+    for h in range(cells // MARGIN):
+        wide_ens[h * local:(h + 1) * local, :] = ens_ref[:, h * MARGIN:(h + 1) * MARGIN].astype(F32)
+    in_column = (lax.broadcasted_iota(jnp.int32, (cells // MARGIN, slots), 0) == column).astype(F32).astype(BF16)
+    in_lane = lax.broadcasted_iota(jnp.int32, (MARGIN, slots), 0) == lane
+    gathered = []
+    for k in range(local):
+        values = wide_ens[pl.ds(k, cells // MARGIN, stride=local), :].astype(BF16)
+        found = dot_tn(values, in_column)
+        gathered.append(jnp.sum(jnp.where(in_lane, found, 0.0), axis=0, keepdims=True))
+    at_buf[rows(me), :] = jnp.concatenate(gathered, axis=0).astype(BF16)
+    bord[region] = ens_ref[:, pl.ds(0, MARGIN)]
+
+    pl.semaphore_wait(barrier, regions + n - 2)
+    up = remote(bl_ref, bl_buf.at[0], bl_send.at[0], bl_recv.at[0], member=lax.rem(me + 1, n))
+    down = remote(bl_ref, bl_buf.at[1], bl_send.at[1], bl_recv.at[1], member=lax.rem(me + n - 1, n))
+    lax.fori_loop(1, regions, started(border_copy), 0)
     lax.fori_loop(1, n, started(at_copy), 0)
+    up.start()
+    down.start()
 
     holder = (target // cells).astype(F32)
     s_low = jnp.min(jnp.where(is_local, 1e6, holder), axis=1, keepdims=True)
     s_high = jnp.max(jnp.where(is_local, -1.0, holder), axis=1, keepdims=True)
-    lax.fori_loop(1, ys, arrived(y_copy), 0)
+    lax.fori_loop(1, regions, arrived(border_copy), 0)
 
     def pick(s, c):
         low, high = c
@@ -175,7 +171,7 @@
         return jnp.where(s_low == at, block, low), jnp.where(s_high == at, block, high)
 
     nothing = jnp.zeros((local, MARGIN), F32)
-    low, high = lax.fori_loop(0, zs * ys, pick, (nothing, nothing))
+    low, high = lax.fori_loop(0, regions, pick, (nothing, nothing), unroll=8)
     mine = jnp.concatenate([low, high], axis=1).astype(BF16)
     fwd[...] = mine
     picked[rows(me), :] = mine
@@ -247,10 +243,9 @@
     for q in range(points):
         m = right(split(1.5 * eye - 0.5 * x_s[q]))
         root = dot(left(split(z_s[q])), m)
-        root_parts = left(split(root))
-        step = dot(root_parts, right(split(forcing_s[...])))
-        mean_weights = dot(root_parts, right(split(step))) * (1.0 / frob[q])
-        t_s[q] = (mean_weights[:, q:q + 1] + (math.sqrt(members - 1.0) * lax.rsqrt(frob[q])) * root).astype(BF16)
+        step = jnp.sum(root * forcing_s[:, q:q + 1], axis=0, keepdims=True)
+        mean_weights = jnp.sum(root * step, axis=1, keepdims=True) * (1.0 / frob[q])
+        t_s[q] = (mean_weights + (math.sqrt(members - 1.0) * lax.rsqrt(frob[q])) * root).astype(BF16)
 
     lax.fori_loop(1, n, arrived(ce_copy), 0)
 
@@ -328,13 +323,7 @@
 
     mine_0 = mean_col[part(0)] + blended(anom[part(0)], 1)
     mine_1 = mean_col[part(half)] + blended(anom[part(half)], 2)
-    out_copy(0, lax.rem(me + 1, n), 0).wait_recv()
-    out_ref[:half] = (mine_0 + got[0].astype(F32)).astype(BF16)
-    out_copy(1, lax.rem(me + n - 1, n), 1).wait_recv()
-    out_ref[half:] = (mine_1 + got[1].astype(F32)).astype(BF16)
-
-    lax.fori_loop(1, zs, sent_off(z_copy), 0)
-    lax.fori_loop(1, ys, sent_off(y_copy), 0)
+    lax.fori_loop(1, regions, sent_off(border_copy), 0)
     lax.fori_loop(1, n, sent_off(at_copy), 0)
     lax.fori_loop(1, n, sent_off(fw_copy), 0)
     lax.fori_loop(1, n, sent_off(ce_copy), 0)
@@ -357,6 +346,11 @@
     def _():
         out_copy(1, me - 1, 1).wait_send()
 
+    out_copy(0, lax.rem(me + 1, n), 0).wait_recv()
+    out_ref[:half] = (mine_0 + got[0].astype(F32)).astype(BF16)
+    out_copy(1, lax.rem(me + n - 1, n), 1).wait_recv()
+    out_ref[half:] = (mine_1 + got[1].astype(F32)).astype(BF16)
+
 
 def per_device(ensemble, reports, report_count, report_cell, report_weight, blending):
     local, cells = ensemble.shape
@@ -366,13 +360,21 @@
     points = report_weight.shape[1]
     half = cells // n // 2
     vmem = pl.BlockSpec(memory_space=pltpu.VMEM)
+    anywhere = pl.BlockSpec(memory_space=pltpu.HBM)
     dma = pltpu.SemaphoreType.DMA
     return pl.pallas_call(
         kernel,
         out_shape=jax.ShapeDtypeStruct((cells // n, members), BF16),
-        in_specs=[pl.BlockSpec(memory_space=pltpu.SMEM)] + [vmem] * 5,
+        in_specs=[anywhere] * 6,
         out_specs=vmem,
         scratch_shapes=[
+            pltpu.SMEM((1,), jnp.int32),
+            pltpu.VMEM((local, cells), BF16),
+            pltpu.VMEM((1, slots), F32),
+            pltpu.VMEM((1, slots), jnp.int32),
+            pltpu.VMEM((points, slots), F32),
+            pltpu.VMEM((4, 2 * half), F32),
+            dma((6,)),
             pltpu.VMEM((members, slots), BF16),
             pltpu.VMEM((members, 4 * half), BF16),
             pltpu.VMEM((members, half), BF16),
@@ -385,15 +387,16 @@
             pltpu.VMEM((4 * half, members), BF16),
             pltpu.VMEM((half, members), BF16),
             pltpu.VMEM((4 * half, 1), F32),
+            pltpu.VMEM((local * cells // MARGIN, MARGIN), F32),
             pltpu.VMEM((points, members, members), F32),
             pltpu.VMEM((points, members, members), F32),
             pltpu.VMEM((points, members, members), BF16),
             pltpu.VMEM((members, MARGIN), F32),
-            dma((4,)), dma((4,)), dma((8,)), dma((8,)), dma((n,)), dma((n,)), dma((n,)), dma((n,)), dma((n,)), dma((n,)),
+            dma((lax.axis_size("region"),)), dma((lax.axis_size("region"),)), dma((n,)), dma((n,)), dma((n,)), dma((n,)), dma((n,)), dma((n,)),
             dma((2,)), dma((2,)), dma((2,)), dma((n,)), dma((3,)), dma((2,)),
         ],
         compiler_params=pltpu.CompilerParams(
-            collective_id=0, has_side_effects=True, vmem_limit_bytes=48 * 1024 * 1024
+            collective_id=0, has_side_effects=True, vmem_limit_bytes=64 * 1024 * 1024
         ),
     )(report_count, ensemble, reports, report_cell, report_weight[0], blending)
 

time: 58.7 us -> 48 us (0.82)
  Pallas kernels: 53.3 us -> 45.5 us
  local copies, waits for them, and re-layouts: 4.43 us -> 1.67 us
    pallas_call x1, Pallas kernels: 53.3 us -> 45.5 us  [per_device(): pl.pallas_call(kernel, out_shape=jax.ShapeDtypeStruct((cells // n, member...]
    unnamed x11 -> x1, local copies, waits for them, and re-layouts: 4.43 us -> 1.67 us
where the time goes in v2:
time: 48 us; the launch traced here: 47.8 us
  Pallas kernels  45.5 us (95%)
  local copies, waits for them, and re-layouts  1.67 us (3%)
  between operations  0.66 us (1%)
    pallas_call x1, Pallas kernels, per_device(): pl.pallas_call(kernel, out_shape=jax.ShapeDtypeStruct((cells // n, member...  45.5 us
    unnamed x1, local copies, waits for them, and re-layouts  1.67 us

profile of v2, /device:TPU:1, one launch (start us, length us, event | category | flops | bytes accessed | tf_op | source)
XLA Modules:
  0.0 47.8 jit_solution(9925199579949932012)
XLA Ops:
  0.7 45.5 %shard_map.64 = bf16[512,256]{1,0:T(8,128)(2,1)} custom-call(s32[1]{0:T(128)S(6)} %copy.8.count_hbm, bf16[16,8192]{1,0:T(8,128)(2,1)} %ens_hbm.1, f32[1,1024]{1,0:T(1,128)} %rep_hbm.1, s32[1,1024]{1,0:T(1,128)} %cell_hbm.1, f32[4,1024]{1,0:T(4,128)} %bitcast.1, f32[4,512]{1,0:T(4,128)} %bl_hbm.1), custom_call_target="tpu_custom_call" | custom-call | tf_op jit(solution)/shard_map/pallas_call | solution.py:365
  46.1 1.7 %copy.9 = bf16[512,256]{1,0:T(8,128)(2,1)} copy(bf16[512,256]{1,0:T(8,128)(2,1)} %shard_map.64) | data formatting | bytes 524288

commit v3 on v2

--- a/solution.py
+++ b/solution.py
@@ -10,6 +10,7 @@
 
 MESH = pl.DeviceIdType.MESH
 MARGIN = 128
+Z_CHIPS = 4
 F32 = jnp.float32
 BF16 = jnp.bfloat16
 
@@ -30,16 +31,6 @@
 
 def dot_tn(a, b):
     return lax.dot_general(a, b, (((0,), (0,)), ((), ())), preferred_element_type=F32)
-
-
-def left(parts):
-    high, low = parts
-    return jnp.concatenate([high, high, low], axis=1)
-
-
-def right(parts):
-    high, low = parts
-    return jnp.concatenate([high, low, high], axis=0)
 
 
 def kernel(
@@ -47,7 +38,7 @@
     count_ref, ens_ref, rep_ref, cell_ref, rw_ref, bl_ref, in_sem,
     at_buf, cells_buf, extra_buf, bl_buf, bord, fwd, picked, sent, got, anom, extra_anom, mean_col,
     wide_ens, x_s, z_s, t_s, forcing_s,
-    bo_send, bo_recv, at_send, at_recv, ce_send, ce_recv, fw_send, fw_recv,
+    bz_send, bz_recv, by_send, by_recv, at_send, at_recv, ce_send, ce_recv, fw_send, fw_recv,
     bl_send, bl_recv, xs_send, xs_recv, cn_send, cn_recv,
 ):
     loads = [
@@ -61,9 +52,12 @@
     region = lax.axis_index("region")
     me = lax.axis_index("member")
     local, cells = ens_ref.shape
+    zs = Z_CHIPS
     n = 16
     members = n * local
     regions = bord.shape[0]
+    ys = regions // zs
+    y, z = region // zs, region % zs
     half = cells // n // 2
     slots = at_buf.shape[1]
     first = (n - 1 - me) // (n - 1)
@@ -72,8 +66,11 @@
     def peer(i):
         return lax.rem(me + i, n)
 
-    def region_peer(i):
-        return lax.rem(region + i, regions)
+    def z_peer(i):
+        return y * zs + lax.rem(z + i, zs)
+
+    def y_peer(i):
+        return lax.rem(y + i, ys) * zs + z
 
     def rows(d):
         return pl.ds(pl.multiple_of(d * local, local), local)
@@ -89,18 +86,27 @@
         pl.semaphore_signal(barrier, inc=1, device_id={"member": peer(i)}, device_id_type=MESH)
         return c
 
-    def greet_region(i, c):
-        pl.semaphore_signal(barrier, inc=1, device_id={"region": region_peer(i)}, device_id_type=MESH)
+    def greet_z(i, c):
+        pl.semaphore_signal(barrier, inc=1, device_id={"region": z_peer(i)}, device_id_type=MESH)
         return c
 
-    lax.fori_loop(1, regions, greet_region, 0)
+    def greet_y(i, c):
+        pl.semaphore_signal(barrier, inc=1, device_id={"region": y_peer(i)}, device_id_type=MESH)
+        return c
+
+    lax.fori_loop(1, zs, greet_z, 0)
+    lax.fori_loop(1, ys, greet_y, 0)
     lax.fori_loop(1, n, greet, 0)
     for load in loads:
         load.wait()
 
-    def border_copy(i):
+    def z_copy(i):
         source = ens_ref.at[:, pl.ds(0, MARGIN)]
-        return remote(source, bord.at[region], bo_send.at[i], bo_recv.at[i], region=region_peer(i))
+        return remote(source, bord.at[region], bz_send.at[i], bz_recv.at[i], region=z_peer(i))
+
+    def y_copy(i):
+        block = bord.at[pl.ds(y * zs, zs)]
+        return remote(block, block, by_send.at[i], by_recv.at[i], region=y_peer(i))
 
     def at_copy(i):
         block = at_buf.at[rows(me)]
@@ -151,18 +157,18 @@
     at_buf[rows(me), :] = jnp.concatenate(gathered, axis=0).astype(BF16)
     bord[region] = ens_ref[:, pl.ds(0, MARGIN)]
 
-    pl.semaphore_wait(barrier, regions + n - 2)
+    pl.semaphore_wait(barrier, zs + ys + n - 3)
     up = remote(bl_ref, bl_buf.at[0], bl_send.at[0], bl_recv.at[0], member=lax.rem(me + 1, n))
     down = remote(bl_ref, bl_buf.at[1], bl_send.at[1], bl_recv.at[1], member=lax.rem(me + n - 1, n))
-    lax.fori_loop(1, regions, started(border_copy), 0)
+    lax.fori_loop(1, zs, started(z_copy), 0)
     lax.fori_loop(1, n, started(at_copy), 0)
-    up.start()
-    down.start()
+    lax.fori_loop(1, zs, arrived(z_copy), 0)
+    lax.fori_loop(1, ys, started(y_copy), 0)
 
     holder = (target // cells).astype(F32)
     s_low = jnp.min(jnp.where(is_local, 1e6, holder), axis=1, keepdims=True)
     s_high = jnp.max(jnp.where(is_local, -1.0, holder), axis=1, keepdims=True)
-    lax.fori_loop(1, regions, arrived(border_copy), 0)
+    lax.fori_loop(1, ys, arrived(y_copy), 0)
 
     def pick(s, c):
         low, high = c
@@ -178,6 +184,8 @@
     lax.fori_loop(1, n, started(fw_copy), 0)
 
     lax.fori_loop(1, n, started(ce_copy), 0)
+    up.start()
+    down.start()
     cells_buf[rows(me), :] = ens_ref[:, pl.ds(cell_start(me), 4 * half)]
 
     def extra_copy(k):
@@ -194,58 +202,80 @@
         def _():
             extra_buf[rows(me), :] = ens_ref[:, pl.ds((0, cells - half)[k], half)]
 
-    lax.fori_loop(1, n, arrived(fw_copy), 0)
-    lax.fori_loop(1, n, arrived(at_copy), 0)
     within = lax.rem(target, cells)
     key = jnp.where(
         is_local, -1,
         jnp.where(holder == s_low, within, jnp.where(holder == s_high, MARGIN + within, -1)),
     )
     onehot = (lax.broadcasted_iota(jnp.int32, (2 * MARGIN, slots), 0) == key).astype(F32).astype(BF16)
-    at_reports = at_buf[...].astype(F32) + dot(picked[...], onehot)
+    active = lax.broadcasted_iota(jnp.int32, (1, slots), 1) < count_ref[0]
+    weights = jnp.where(active, rw_ref[...], 0.0)
+    points = weights.shape[0]
+    pair = jnp.concatenate([weights, weights * rep_ref[...]], axis=0)
+    by_cell = dot_nt(jnp.concatenate(split(pair), axis=0), onehot)
+    by_cell = by_cell[:2 * points] + by_cell[2 * points:]
+    cell_weights, cell_reports = by_cell[:points], by_cell[points:]
+    padding = jnp.zeros((MARGIN - points, slots), F32)
+
+    lax.fori_loop(1, n, arrived(at_copy), 0)
+    at_reports = at_buf[...].astype(F32)
     mean = jnp.sum(at_reports, axis=0, keepdims=True) * (1.0 / members)
     pert = (at_reports - mean).astype(BF16)
     pert_wide = pert.astype(F32)
-    active = lax.broadcasted_iota(jnp.int32, (1, slots), 1) < count_ref[0]
-    weights = jnp.where(active, rw_ref[...], 0.0)
-    points = weights.shape[0]
-    departure = weights * (rep_ref[...] - mean)
-    departure = jnp.concatenate([departure, jnp.zeros((MARGIN - points, slots), F32)], axis=0).astype(BF16)
+    departure = jnp.concatenate([weights * (rep_ref[...] - mean), padding], axis=0).astype(BF16)
     forcing_s[...] = dot_nt(pert, departure)
+    for q in range(points):
+        x_s[q] = dot_nt((pert_wide * weights[q:q + 1]).astype(BF16), pert)
+
+    lax.fori_loop(1, n, arrived(fw_copy), 0)
+    values = picked[...].astype(F32)
+    mean = jnp.sum(values, axis=0, keepdims=True) * (1.0 / members)
+    pert = (values - mean).astype(BF16)
+    pert_wide = pert.astype(F32)
+    departure = jnp.concatenate([cell_reports - cell_weights * mean, padding[:, :2 * MARGIN]], axis=0).astype(BF16)
+    forcing = forcing_s[...] + dot_nt(pert, departure)
     eye = (
         lax.broadcasted_iota(jnp.int32, (members, members), 0)
         == lax.broadcasted_iota(jnp.int32, (members, members), 1)
     ).astype(F32)
-    frob = []
+
+    def total(v):
+        return jnp.sum(jnp.sum(v, axis=0, keepdims=True), axis=1, keepdims=True)
+
+    scales = []
     for q in range(points):
-        weighted = (pert_wide * weights[q:q + 1]).astype(BF16)
-        precision_mat = (members - 1.0) * eye + dot_nt(weighted, pert)
-        squares = jnp.sum(jnp.sum(precision_mat * precision_mat, axis=0, keepdims=True), axis=1, keepdims=True)
-        f = jnp.sqrt(squares)
-        frob.append(f)
-        a = precision_mat * (1.0 / f)
-        middle = 1.5 * eye - 0.5 * a
-        m = right(split(middle))
-        inner = dot(left(split(a)), m)
-        x_s[q] = dot(left(split(inner)), m)
-        z_s[q] = middle
-
-    def sweep(i, c):
+        weighted = (pert_wide * cell_weights[q:q + 1]).astype(BF16)
+        precision_mat = (members - 1.0) * eye + x_s[q] + dot_nt(weighted, pert)
+        frob = jnp.sqrt(total(precision_mat * precision_mat))
+        c = total(precision_mat * eye) * (1.0 / members) / frob
+        x_s[q] = precision_mat * (1.0 / frob) - c * eye
+        scales.append((frob, c))
+
+    centres = [c for _, c in scales]
+    gains = [1.0 for _ in scales]
+    for sweep in range(4):
         for q in range(points):
-            x = x_s[q]
-            m = right(split(1.5 * eye - 0.5 * x))
-            inner = dot(left(split(x)), m)
-            z_s[q] = dot(left(split(z_s[q])), m)
-            x_s[q] = dot(left(split(inner)), m)
-        return c
-
-    lax.fori_loop(0, 2, sweep, 0)
+            e_part = x_s[q]
+            narrow_e = e_part.astype(BF16)
+            c, g = centres[q], gains[q]
+            d = 1.5 - 0.5 * c
+            if sweep:
+                j_part = z_s[q]
+                j_next = d * j_part - (0.5 * g) * e_part - 0.5 * dot(j_part.astype(BF16), narrow_e)
+            else:
+                j_next = -0.5 * e_part
+            gains[q] = g * d
+            if sweep < 3:
+                h_part = (d - 0.5 * c) * e_part - 0.5 * dot(narrow_e, narrow_e)
+                x_s[q] = d * h_part - (0.5 * c * d) * e_part - 0.5 * dot(h_part.astype(BF16), narrow_e)
+                centres[q] = c * d * d
+            z_s[q] = j_next
     for q in range(points):
-        m = right(split(1.5 * eye - 0.5 * x_s[q]))
-        root = dot(left(split(z_s[q])), m)
-        step = jnp.sum(root * forcing_s[:, q:q + 1], axis=0, keepdims=True)
-        mean_weights = jnp.sum(root * step, axis=1, keepdims=True) * (1.0 / frob[q])
-        t_s[q] = (mean_weights + (math.sqrt(members - 1.0) * lax.rsqrt(frob[q])) * root).astype(BF16)
+        root = gains[q] * eye + z_s[q]
+        frob = scales[q][0]
+        step = jnp.sum(root * forcing[:, q:q + 1], axis=0, keepdims=True)
+        mean_weights = jnp.sum(root * step, axis=1, keepdims=True) * (1.0 / frob)
+        t_s[q] = (mean_weights + (math.sqrt(members - 1.0) * lax.rsqrt(frob)) * root).astype(BF16)
 
     lax.fori_loop(1, n, arrived(ce_copy), 0)
 
@@ -323,7 +353,8 @@
 
     mine_0 = mean_col[part(0)] + blended(anom[part(0)], 1)
     mine_1 = mean_col[part(half)] + blended(anom[part(half)], 2)
-    lax.fori_loop(1, regions, sent_off(border_copy), 0)
+    lax.fori_loop(1, zs, sent_off(z_copy), 0)
+    lax.fori_loop(1, ys, sent_off(y_copy), 0)
     lax.fori_loop(1, n, sent_off(at_copy), 0)
     lax.fori_loop(1, n, sent_off(fw_copy), 0)
     lax.fori_loop(1, n, sent_off(ce_copy), 0)
@@ -357,6 +388,7 @@
     n = lax.axis_size("member")
     members = n * local
     slots = reports.shape[1]
+    regions, zs = lax.axis_size("region"), Z_CHIPS
     points = report_weight.shape[1]
     half = cells // n // 2
     vmem = pl.BlockSpec(memory_space=pltpu.VMEM)
@@ -379,7 +411,7 @@
             pltpu.VMEM((members, 4 * half), BF16),
             pltpu.VMEM((members, half), BF16),
             pltpu.VMEM((2, 4, 2 * half), F32),
-            pltpu.VMEM((lax.axis_size("region"), local, MARGIN), BF16),
+            pltpu.VMEM((regions, local, MARGIN), BF16),
             pltpu.VMEM((local, 2 * MARGIN), BF16),
             pltpu.VMEM((members, 2 * MARGIN), BF16),
             pltpu.VMEM((3, half, members), BF16),
@@ -392,13 +424,13 @@
             pltpu.VMEM((points, members, members), F32),
             pltpu.VMEM((points, members, members), BF16),
             pltpu.VMEM((members, MARGIN), F32),
-            dma((lax.axis_size("region"),)), dma((lax.axis_size("region"),)), dma((n,)), dma((n,)), dma((n,)), dma((n,)), dma((n,)), dma((n,)),
+            dma((zs,)), dma((zs,)), dma((regions // zs,)), dma((regions // zs,)), dma((n,)), dma((n,)), dma((n,)), dma((n,)), dma((n,)), dma((n,)),
             dma((2,)), dma((2,)), dma((2,)), dma((n,)), dma((3,)), dma((2,)),
         ],
         compiler_params=pltpu.CompilerParams(
-            collective_id=0, has_side_effects=True, vmem_limit_bytes=64 * 1024 * 1024
+            collective_id=0, has_side_effects=True, vmem_limit_bytes=48 * 1024 * 1024
         ),
-    )(report_count, ensemble, reports, report_cell, report_weight[0], blending)
+    )(report_count, *(pltpu.with_memory_space_constraint(v, pltpu.HBM) for v in (ensemble, reports, report_cell, report_weight[0], blending)))
 
 
 def solution(mesh):

time: 48 us -> 41.7 us (0.87)
  Pallas kernels: 45.5 us -> 40.2 us
  local copies, waits for them, and re-layouts: 1.67 us -> 0.71 us
    pallas_call x1, Pallas kernels: 45.5 us -> 40.2 us  [per_device(): pl.pallas_call(kernel, out_shape=jax.ShapeDtypeStruct((cells // n, member...]
    unnamed x1, local copies, waits for them, and re-layouts: 1.67 us -> 0.71 us
where the time goes in v3:
time: 41.7 us; the launch traced here: 41.6 us
  Pallas kernels  40.2 us (96%)
  local copies, waits for them, and re-layouts  0.71 us (2%)
  between operations  0.66 us (2%)
    pallas_call x1, Pallas kernels, per_device(): pl.pallas_call(kernel, out_shape=jax.ShapeDtypeStruct((cells // n, member...  40.2 us

profile of v3, /device:TPU:1, one launch (start us, length us, event | category | flops | bytes accessed | tf_op | source)
XLA Modules:
  0.0 41.6 jit_solution(13897795187909007503)
XLA Ops:
  0.7 40.2 %shard_map.64 = bf16[512,256]{1,0:T(8,128)(2,1)S(1)} custom-call(s32[1]{0:T(128)S(6)} %copy.8.count_hbm, bf16[16,8192]{1,0:T(8,128)(2,1)} %ens_hbm.1, f32[1,1024]{1,0:T(1,128)} %rep_hbm.1, s32[1,1024]{1,0:T(1,128)} %cell_hbm.1, f32[4,1024]{1,0:T(4,128)} %bitcast.1, f32[4,512]{1,0:T(4,128)} %bl_hbm.1), custom_call_target="tpu_custom_call" | custom-call | tf_op jit(solution)/shard_map/pallas_call | solution.py:397
  40.9 0.7 %copy.9 = bf16[512,256]{1,0:T(8,128)(2,1)} copy(bf16[512,256]{1,0:T(8,128)(2,1)S(1)} %shard_map.64) | data formatting | bytes 524288

commit v4 on v3

--- a/solution.py
+++ b/solution.py
@@ -36,19 +36,11 @@
 def kernel(
     count_hbm, ens_hbm, rep_hbm, cell_hbm, rw_hbm, bl_hbm, out_ref,
     count_ref, ens_ref, rep_ref, cell_ref, rw_ref, bl_ref, in_sem,
-    at_buf, cells_buf, extra_buf, bl_buf, bord, fwd, picked, sent, got, anom, extra_anom, mean_col,
+    at_buf, cells_buf, extra_buf, bl_buf, bord, fwd, picked, sent, got, mix_s,
     wide_ens, x_s, z_s, t_s, forcing_s,
-    bz_send, bz_recv, by_send, by_recv, at_send, at_recv, ce_send, ce_recv, fw_send, fw_recv,
+    by_send, by_recv, dn_send, dn_recv, pu_send, pu_recv, ready, at_send, at_recv, ce_send, ce_recv, fw_send, fw_recv,
     bl_send, bl_recv, xs_send, xs_recv, cn_send, cn_recv,
 ):
-    loads = [
-        pltpu.make_async_copy(source, landed, in_sem.at[i])
-        for i, (source, landed) in enumerate((
-            (cell_hbm, cell_ref), (ens_hbm, ens_ref), (bl_hbm, bl_ref), (rw_hbm, rw_ref), (rep_hbm, rep_ref), (count_hbm, count_ref)
-        ))
-    ]
-    for load in loads:
-        load.start()
     region = lax.axis_index("region")
     me = lax.axis_index("member")
     local, cells = ens_ref.shape
@@ -66,11 +58,13 @@
     def peer(i):
         return lax.rem(me + i, n)
 
-    def z_peer(i):
-        return y * zs + lax.rem(z + i, zs)
+    later = zs - 1 - z
+
+    def at_row(i, plane):
+        return lax.rem(y + i, ys) * zs + plane
 
     def y_peer(i):
-        return lax.rem(y + i, ys) * zs + z
+        return at_row(i, z)
 
     def rows(d):
         return pl.ds(pl.multiple_of(d * local, local), local)
@@ -80,33 +74,29 @@
             src_ref=src, dst_ref=dst, send_sem=ss, recv_sem=rs, device_id=where, device_id_type=MESH
         )
 
-    barrier = pltpu.get_barrier_semaphore()
-
-    def greet(i, c):
-        pl.semaphore_signal(barrier, inc=1, device_id={"member": peer(i)}, device_id_type=MESH)
-        return c
-
-    def greet_z(i, c):
-        pl.semaphore_signal(barrier, inc=1, device_id={"region": z_peer(i)}, device_id_type=MESH)
-        return c
-
-    def greet_y(i, c):
-        pl.semaphore_signal(barrier, inc=1, device_id={"region": y_peer(i)}, device_id_type=MESH)
-        return c
-
-    lax.fori_loop(1, zs, greet_z, 0)
-    lax.fori_loop(1, ys, greet_y, 0)
-    lax.fori_loop(1, n, greet, 0)
-    for load in loads:
-        load.wait()
-
-    def z_copy(i):
-        source = ens_ref.at[:, pl.ds(0, MARGIN)]
-        return remote(source, bord.at[region], bz_send.at[i], bz_recv.at[i], region=z_peer(i))
+    own_block = z * ys + y
+    edge_hbm = ens_hbm.at[:, pl.ds(0, MARGIN)]
+    own_plane = bord.at[pl.ds(z * ys, ys)]
 
     def y_copy(i):
-        block = bord.at[pl.ds(y * zs, zs)]
-        return remote(block, block, by_send.at[i], by_recv.at[i], region=y_peer(i))
+        return remote(edge_hbm, bord.at[own_block], by_send.at[i], by_recv.at[i], region=y_peer(i))
+
+    def down_copy(t):
+        where = at_row(lax.rem(t, ys), z - t // ys)
+        return remote(edge_hbm, bord.at[own_block], dn_send.at[t], dn_recv.at[t], region=where)
+
+    def start_down(t, c):
+        down_copy(ys * (z - t // ys) + lax.rem(t, ys)).start()
+        return c
+
+    def down_arrival(t):
+        return remote(edge_hbm, bord.at[own_block], dn_send.at[t], dn_recv.at[t], region=y_peer(1))
+
+    def up_copy(k):
+        return remote(own_plane, own_plane, pu_send.at[k], pu_recv.at[k], region=y * zs + z + k)
+
+    def up_arrival(k):
+        return remote(own_plane, own_plane, pu_send.at[k], pu_recv.at[k], region=y_peer(1))
 
     def at_copy(i):
         block = at_buf.at[rows(me)]
@@ -139,6 +129,44 @@
             copy(i).wait_recv()
             return c
         return body
+
+    barrier = pltpu.get_barrier_semaphore()
+
+    def greet(i, c):
+        pl.semaphore_signal(barrier, inc=1, device_id={"member": peer(i)}, device_id_type=MESH)
+        return c
+
+    def greet_later(t, c):
+        where = at_row(lax.rem(t, ys), z + t // ys)
+        pl.semaphore_signal(barrier, inc=1, device_id={"region": where}, device_id_type=MESH)
+        return c
+
+    def say_ready(k, c):
+        pl.semaphore_signal(ready.at[k], inc=1, device_id={"region": y * zs + z - k}, device_id_type=MESH)
+        return c
+
+    def greet_y(i, c):
+        pl.semaphore_signal(barrier, inc=1, device_id={"region": y_peer(i)}, device_id_type=MESH)
+        return c
+
+    lax.fori_loop(1, ys, greet_y, 0)
+    lax.fori_loop(1, n, greet, 0)
+    loads = [
+        pltpu.make_async_copy(source, landed, in_sem.at[i])
+        for i, (source, landed) in enumerate((
+            (ens_hbm, ens_ref), (cell_hbm, cell_ref), (bl_hbm, bl_ref), (rw_hbm, rw_ref), (rep_hbm, rep_ref), (count_hbm, count_ref)
+        ))
+    ]
+    for load in loads:
+        load.start()
+    lax.fori_loop(ys, ys + ys * later, greet_later, 0)
+    pl.semaphore_wait(barrier, ys + n - 2 + ys * z)
+    lax.fori_loop(1, 1 + z, say_ready, 0)
+    lax.fori_loop(0, ys * z, start_down, 0)
+    lax.fori_loop(1, ys, started(y_copy), 0)
+    for load in loads:
+        load.wait()
+    bord[own_block] = ens_ref[:, pl.ds(0, MARGIN)]
 
     target = cell_ref[...]
     relative = target - region * cells
@@ -155,37 +183,54 @@
         found = dot_tn(values, in_column)
         gathered.append(jnp.sum(jnp.where(in_lane, found, 0.0), axis=0, keepdims=True))
     at_buf[rows(me), :] = jnp.concatenate(gathered, axis=0).astype(BF16)
-    bord[region] = ens_ref[:, pl.ds(0, MARGIN)]
-
-    pl.semaphore_wait(barrier, zs + ys + n - 3)
+
     up = remote(bl_ref, bl_buf.at[0], bl_send.at[0], bl_recv.at[0], member=lax.rem(me + 1, n))
     down = remote(bl_ref, bl_buf.at[1], bl_send.at[1], bl_recv.at[1], member=lax.rem(me + n - 1, n))
-    lax.fori_loop(1, zs, started(z_copy), 0)
+    up.start()
+    down.start()
     lax.fori_loop(1, n, started(at_copy), 0)
-    lax.fori_loop(1, zs, arrived(z_copy), 0)
-    lax.fori_loop(1, ys, started(y_copy), 0)
+    lax.fori_loop(1, n, started(ce_copy), 0)
 
     holder = (target // cells).astype(F32)
     s_low = jnp.min(jnp.where(is_local, 1e6, holder), axis=1, keepdims=True)
     s_high = jnp.max(jnp.where(is_local, -1.0, holder), axis=1, keepdims=True)
-    lax.fori_loop(1, ys, arrived(y_copy), 0)
-
-    def pick(s, c):
-        low, high = c
-        block = bord[s].astype(F32)
-        at = s.astype(F32)
+
+    def pick(plane, row, found):
+        low, high = found
+        block = bord[plane * ys + row].astype(F32)
+        at = (row * zs + plane).astype(F32)
         return jnp.where(s_low == at, block, low), jnp.where(s_high == at, block, high)
 
+    def pick_row(i, found):
+        y_copy(i).wait_recv()
+        return pick(z, lax.rem(y + ys - i, ys), found)
+
+    def send_up(k, c):
+        pl.semaphore_wait(ready.at[k], 1)
+        up_copy(k).start()
+        return c
+
+    def pick_later(t, found):
+        down_arrival(t).wait_recv()
+        return pick(z + t // ys, lax.rem(y + ys - lax.rem(t, ys), ys), found)
+
+    def pick_earlier(k, found):
+        up_arrival(k).wait_recv()
+        for row in range(ys):
+            found = pick(z - k, row, found)
+        return found
+
     nothing = jnp.zeros((local, MARGIN), F32)
-    low, high = lax.fori_loop(0, regions, pick, (nothing, nothing), unroll=8)
+    found = pick(z, y, (nothing, nothing))
+    found = lax.fori_loop(1, ys, pick_row, found)
+    lax.fori_loop(1, 1 + later, send_up, 0)
+    found = lax.fori_loop(ys, ys + ys * later, pick_later, found)
+    low, high = lax.fori_loop(1, 1 + z, pick_earlier, found)
     mine = jnp.concatenate([low, high], axis=1).astype(BF16)
     fwd[...] = mine
     picked[rows(me), :] = mine
     lax.fori_loop(1, n, started(fw_copy), 0)
 
-    lax.fori_loop(1, n, started(ce_copy), 0)
-    up.start()
-    down.start()
     cells_buf[rows(me), :] = ens_ref[:, pl.ds(cell_start(me), 4 * half)]
 
     def extra_copy(k):
@@ -227,6 +272,23 @@
     for q in range(points):
         x_s[q] = dot_nt((pert_wide * weights[q:q + 1]).astype(BF16), pert)
 
+    up.wait_recv()
+    down.wait_recv()
+
+    def mixed(values):
+        return values * (1.0 / jnp.sum(values, axis=0, keepdims=True))
+
+    own, below, above = mixed(bl_ref[...]), mixed(bl_buf[0]), mixed(bl_buf[1])
+    weights_of = [
+        below[2:4, half:],
+        jnp.where(me == 0, own[0:2, :half], own[2:4, :half]),
+        jnp.where(me == n - 1, own[2:4, half:], own[0:2, half:]),
+        above[0:2, :half],
+        jnp.where(me == 1, below[2:4, :half], above[0:2, half:]),
+    ]
+    stacked = jnp.concatenate(weights_of + [jnp.zeros((MARGIN - 10, half), F32)], axis=0)
+    mix_s[...] = stacked.T
+
     lax.fori_loop(1, n, arrived(fw_copy), 0)
     values = picked[...].astype(F32)
     mean = jnp.sum(values, axis=0, keepdims=True) * (1.0 / members)
@@ -242,40 +304,42 @@
     def total(v):
         return jnp.sum(jnp.sum(v, axis=0, keepdims=True), axis=1, keepdims=True)
 
-    scales = []
+    block_eye = eye[:MARGIN, :MARGIN]
+    frobs, centres = [], []
     for q in range(points):
         weighted = (pert_wide * cell_weights[q:q + 1]).astype(BF16)
         precision_mat = (members - 1.0) * eye + x_s[q] + dot_nt(weighted, pert)
+        trace = sum(
+            total(precision_mat[k:k + MARGIN, k:k + MARGIN] * block_eye) for k in range(0, members, MARGIN)
+        ) * (1.0 / members)
         frob = jnp.sqrt(total(precision_mat * precision_mat))
-        c = total(precision_mat * eye) * (1.0 / members) / frob
-        x_s[q] = precision_mat * (1.0 / frob) - c * eye
-        scales.append((frob, c))
-
-    centres = [c for _, c in scales]
-    gains = [1.0 for _ in scales]
+        x_s[q] = precision_mat * (1.0 / trace) - eye
+        frobs.append(frob)
+        centres.append(trace / frob)
+
+    gains = [1.0 for _ in frobs]
     for sweep in range(4):
         for q in range(points):
-            e_part = x_s[q]
-            narrow_e = e_part.astype(BF16)
-            c, g = centres[q], gains[q]
-            d = 1.5 - 0.5 * c
+            f_part = x_s[q]
+            d = 1.5 - 0.5 * centres[q]
+            away = (0.5 * centres[q] / d) * f_part
+            narrow = away.astype(BF16)
             if sweep:
-                j_part = z_s[q]
-                j_next = d * j_part - (0.5 * g) * e_part - 0.5 * dot(j_part.astype(BF16), narrow_e)
+                k_part = z_s[q]
+                z_s[q] = k_part - away - dot(k_part.astype(BF16), narrow)
             else:
-                j_next = -0.5 * e_part
-            gains[q] = g * d
+                z_s[q] = -away
             if sweep < 3:
-                h_part = (d - 0.5 * c) * e_part - 0.5 * dot(narrow_e, narrow_e)
-                x_s[q] = d * h_part - (0.5 * c * d) * e_part - 0.5 * dot(h_part.astype(BF16), narrow_e)
-                centres[q] = c * d * d
-            z_s[q] = j_next
+                h_part = f_part - away - dot(f_part.astype(BF16), narrow)
+                x_s[q] = h_part - away - dot(h_part.astype(BF16), narrow)
+            gains[q] = gains[q] * d
+            centres[q] = centres[q] * d * d
     for q in range(points):
-        root = gains[q] * eye + z_s[q]
-        frob = scales[q][0]
+        root = eye + z_s[q]
+        frob, gain = frobs[q], gains[q]
         step = jnp.sum(root * forcing[:, q:q + 1], axis=0, keepdims=True)
-        mean_weights = jnp.sum(root * step, axis=1, keepdims=True) * (1.0 / frob)
-        t_s[q] = (mean_weights + (math.sqrt(members - 1.0) * lax.rsqrt(frob)) * root).astype(BF16)
+        mean_weights = jnp.sum(root * step, axis=1, keepdims=True) * (gain * gain / frob)
+        t_s[q] = (mean_weights + (math.sqrt(members - 1.0) * gain * lax.rsqrt(frob)) * root).astype(BF16)
 
     lax.fori_loop(1, n, arrived(ce_copy), 0)
 
@@ -284,26 +348,7 @@
         mean = jnp.sum(across, axis=1, keepdims=True) * (1.0 / members)
         return mean, (across - mean).astype(BF16)
 
-    for b in range(4):
-        cut = slice(b * half, (b + 1) * half)
-        mean_col[cut], anom[cut] = turn(cells_buf[:, cut])
-
-    up.wait_recv()
-    down.wait_recv()
-
-    def mixed(values):
-        return values * (1.0 / jnp.sum(values, axis=0, keepdims=True))
-
-    own, below, above = mixed(bl_ref[...]), mixed(bl_buf[0]), mixed(bl_buf[1])
-    weights_of = [
-        below[2:4, half:],
-        jnp.where(me == 0, own[0:2, :half], own[2:4, :half]),
-        jnp.where(me == n - 1, own[2:4, half:], own[0:2, half:]),
-        above[0:2, :half],
-        jnp.where(me == 1, below[2:4, :half], above[0:2, half:]),
-    ]
-    stacked = jnp.concatenate(weights_of + [jnp.zeros((MARGIN - 10, half), F32)], axis=0)
-    mix = stacked.T
+    mix = mix_s[...]
 
     narrow, wide = 3 * half // 8, 5 * half // 8
 
@@ -329,12 +374,12 @@
 
     @pl.when(me < n - 1)
     def _():
-        sent[0] = blended(anom[part(2 * half)], 3).astype(BF16)
+        sent[0] = blended(turn(cells_buf[:, part(2 * half)])[1], 3).astype(BF16)
         out_copy(0, me + 1, 0).start()
 
     @pl.when(me > 0)
     def _():
-        sent[1] = blended(anom[part(-half)], 0).astype(BF16)
+        sent[1] = blended(turn(cells_buf[:, part(-half)])[1], 0).astype(BF16)
         out_copy(1, me - 1, 1).start()
 
     for k, d, target_d, side in ((0, 1, 0, 0), (1, n - 2, n - 1, 1)):
@@ -351,10 +396,14 @@
             sent[2] = blended(turn(extra_buf[...])[1], 4).astype(BF16)
             out_copy(2, target_d, side).start()
 
-    mine_0 = mean_col[part(0)] + blended(anom[part(0)], 1)
-    mine_1 = mean_col[part(half)] + blended(anom[part(half)], 2)
-    lax.fori_loop(1, zs, sent_off(z_copy), 0)
+    cell_mean, anomaly = turn(cells_buf[:, part(0)])
+    mine_0 = cell_mean + blended(anomaly, 1)
+    cell_mean, anomaly = turn(cells_buf[:, part(half)])
+    mine_1 = cell_mean + blended(anomaly, 2)
+
     lax.fori_loop(1, ys, sent_off(y_copy), 0)
+    lax.fori_loop(ys, ys + ys * z, sent_off(down_copy), 0)
+    lax.fori_loop(1, 1 + later, sent_off(up_copy), 0)
     lax.fori_loop(1, n, sent_off(at_copy), 0)
     lax.fori_loop(1, n, sent_off(fw_copy), 0)
     lax.fori_loop(1, n, sent_off(ce_copy), 0)
@@ -416,15 +465,14 @@
             pltpu.VMEM((members, 2 * MARGIN), BF16),
             pltpu.VMEM((3, half, members), BF16),
             pltpu.VMEM((2, half, members), BF16),
-            pltpu.VMEM((4 * half, members), BF16),
-            pltpu.VMEM((half, members), BF16),
-            pltpu.VMEM((4 * half, 1), F32),
+            pltpu.VMEM((half, MARGIN), F32),
             pltpu.VMEM((local * cells // MARGIN, MARGIN), F32),
             pltpu.VMEM((points, members, members), F32),
             pltpu.VMEM((points, members, members), F32),
             pltpu.VMEM((points, members, members), BF16),
             pltpu.VMEM((members, MARGIN), F32),
-            dma((zs,)), dma((zs,)), dma((regions // zs,)), dma((regions // zs,)), dma((n,)), dma((n,)), dma((n,)), dma((n,)), dma((n,)), dma((n,)),
+            dma((regions // zs,)), dma((regions // zs,)), dma((regions,)), dma((regions,)), dma((zs,)), dma((zs,)),
+            pltpu.SemaphoreType.REGULAR((zs,)), dma((n,)), dma((n,)), dma((n,)), dma((n,)), dma((n,)), dma((n,)),
             dma((2,)), dma((2,)), dma((2,)), dma((n,)), dma((3,)), dma((2,)),
         ],
         compiler_params=pltpu.CompilerParams(

time: 41.7 us -> 41.2 us (0.988)
  Pallas kernels: 40.2 us -> 39.5 us
    pallas_call x1, Pallas kernels: 40.2 us -> 39.5 us  [per_device(): pl.pallas_call(kernel, out_shape=jax.ShapeDtypeStruct((cells // n, member...]
where the time goes in v4:
time: 41.2 us; the launch traced here: 40.8 us
  Pallas kernels  39.5 us (96%)
  local copies, waits for them, and re-layouts  0.71 us (2%)
  between operations  0.66 us (2%)
    pallas_call x1, Pallas kernels, per_device(): pl.pallas_call(kernel, out_shape=jax.ShapeDtypeStruct((cells // n, member...  39.5 us

profile of v4, /device:TPU:1, one launch (start us, length us, event | category | flops | bytes accessed | tf_op | source)
XLA Modules:
  0.0 40.8 jit_solution(7332872666421597047)
XLA Ops:
  0.7 39.5 %shard_map.64 = bf16[512,256]{1,0:T(8,128)(2,1)S(1)} custom-call(s32[1]{0:T(128)S(6)} %copy.8.count_hbm, bf16[16,8192]{1,0:T(8,128)(2,1)} %ens_hbm.1, f32[1,1024]{1,0:T(1,128)} %rep_hbm.1, s32[1,1024]{1,0:T(1,128)} %cell_hbm.1, f32[4,1024]{1,0:T(4,128)} %bitcast.1, f32[4,512]{1,0:T(4,128)} %bl_hbm.1), custom_call_target="tpu_custom_call" | custom-call | tf_op jit(solution)/shard_map/pallas_call | solution.py:446
  40.1 0.7 %copy.9 = bf16[512,256]{1,0:T(8,128)(2,1)} copy(bf16[512,256]{1,0:T(8,128)(2,1)S(1)} %shard_map.64) | data formatting | bytes 524288

commit v5 on v4

--- a/solution.py
+++ b/solution.py
@@ -59,6 +59,7 @@
         return lax.rem(me + i, n)
 
     later = zs - 1 - z
+    lowest = later // (zs - 1)
 
     def at_row(i, plane):
         return lax.rem(y + i, ys) * zs + plane
@@ -189,17 +190,19 @@
     up.start()
     down.start()
     lax.fori_loop(1, n, started(at_copy), 0)
-    lax.fori_loop(1, n, started(ce_copy), 0)
+    lax.fori_loop(1, 1 + (n - 1) * lowest, started(ce_copy), 0)
 
     holder = (target // cells).astype(F32)
     s_low = jnp.min(jnp.where(is_local, 1e6, holder), axis=1, keepdims=True)
     s_high = jnp.max(jnp.where(is_local, -1.0, holder), axis=1, keepdims=True)
+    wide_low = jnp.broadcast_to(s_low.astype(jnp.int32), (local, MARGIN))
+    wide_high = jnp.broadcast_to(s_high.astype(jnp.int32), (local, MARGIN))
 
     def pick(plane, row, found):
         low, high = found
         block = bord[plane * ys + row].astype(F32)
-        at = (row * zs + plane).astype(F32)
-        return jnp.where(s_low == at, block, low), jnp.where(s_high == at, block, high)
+        at = row * zs + plane
+        return jnp.where(wide_low == at, block, low), jnp.where(wide_high == at, block, high)
 
     def pick_row(i, found):
         y_copy(i).wait_recv()
@@ -230,6 +233,7 @@
     fwd[...] = mine
     picked[rows(me), :] = mine
     lax.fori_loop(1, n, started(fw_copy), 0)
+    lax.fori_loop(1, n - (n - 1) * lowest, started(ce_copy), 0)
 
     cells_buf[rows(me), :] = ens_ref[:, pl.ds(cell_start(me), 4 * half)]
 

time: 41.2 us -> 41 us (level)
  no operation moved by 1% of the time
where the time goes in v5:
time: 41 us; the launch traced here: 40.8 us
  Pallas kernels  39.5 us (96%)
  local copies, waits for them, and re-layouts  0.71 us (2%)
  between operations  0.66 us (2%)
    pallas_call x1, Pallas kernels, per_device(): pl.pallas_call(kernel, out_shape=jax.ShapeDtypeStruct((cells // n, member...  39.5 us

profile of v5, /device:TPU:1, one launch (start us, length us, event | category | flops | bytes accessed | tf_op | source)
XLA Modules:
  0.0 40.8 jit_solution(15472898809050537042)
XLA Ops:
  0.7 39.5 %shard_map.64 = bf16[512,256]{1,0:T(8,128)(2,1)S(1)} custom-call(s32[1]{0:T(128)S(6)} %copy.8.count_hbm, bf16[16,8192]{1,0:T(8,128)(2,1)} %ens_hbm.1, f32[1,1024]{1,0:T(1,128)} %rep_hbm.1, s32[1,1024]{1,0:T(1,128)} %cell_hbm.1, f32[4,1024]{1,0:T(4,128)} %bitcast.1, f32[4,512]{1,0:T(4,128)} %bl_hbm.1), custom_call_target="tpu_custom_call" | custom-call | tf_op jit(solution)/shard_map/pallas_call | solution.py:450
  40.1 0.7 %copy.9 = bf16[512,256]{1,0:T(8,128)(2,1)} copy(bf16[512,256]{1,0:T(8,128)(2,1)S(1)} %shard_map.64) | data formatting | bytes 524288

commit v6 on v5

--- a/solution.py
+++ b/solution.py
@@ -59,7 +59,6 @@
         return lax.rem(me + i, n)
 
     later = zs - 1 - z
-    lowest = later // (zs - 1)
 
     def at_row(i, plane):
         return lax.rem(y + i, ys) * zs + plane
@@ -190,7 +189,6 @@
     up.start()
     down.start()
     lax.fori_loop(1, n, started(at_copy), 0)
-    lax.fori_loop(1, 1 + (n - 1) * lowest, started(ce_copy), 0)
 
     holder = (target // cells).astype(F32)
     s_low = jnp.min(jnp.where(is_local, 1e6, holder), axis=1, keepdims=True)
@@ -233,7 +231,7 @@
     fwd[...] = mine
     picked[rows(me), :] = mine
     lax.fori_loop(1, n, started(fw_copy), 0)
-    lax.fori_loop(1, n - (n - 1) * lowest, started(ce_copy), 0)
+    lax.fori_loop(1, n, started(ce_copy), 0)
 
     cells_buf[rows(me), :] = ens_ref[:, pl.ds(cell_start(me), 4 * half)]
 

time: 41 us -> 39.1 us (0.954)
  Pallas kernels: 39.5 us -> 37.6 us
    pallas_call x1, Pallas kernels: 39.5 us -> 37.6 us  [per_device(): pl.pallas_call(kernel, out_shape=jax.ShapeDtypeStruct((cells // n, member...]
where the time goes in v6:
time: 39.1 us; the launch traced here: 39 us
  Pallas kernels  37.6 us (96%)
  local copies, waits for them, and re-layouts  0.71 us (2%)
  between operations  0.66 us (2%)
    pallas_call x1, Pallas kernels, per_device(): pl.pallas_call(kernel, out_shape=jax.ShapeDtypeStruct((cells // n, member...  37.6 us

profile of v6, /device:TPU:1, one launch (start us, length us, event | category | flops | bytes accessed | tf_op | source)
XLA Modules:
  0.0 39.0 jit_solution(795205567359597854)
XLA Ops:
  0.7 37.6 %shard_map.64 = bf16[512,256]{1,0:T(8,128)(2,1)S(1)} custom-call(s32[1]{0:T(128)S(6)} %copy.8.count_hbm, bf16[16,8192]{1,0:T(8,128)(2,1)} %ens_hbm.1, f32[1,1024]{1,0:T(1,128)} %rep_hbm.1, s32[1,1024]{1,0:T(1,128)} %cell_hbm.1, f32[4,1024]{1,0:T(4,128)} %bitcast.1, f32[4,512]{1,0:T(4,128)} %bl_hbm.1), custom_call_target="tpu_custom_call" | custom-call | tf_op jit(solution)/shard_map/pallas_call | solution.py:448
  38.3 0.7 %copy.9 = bf16[512,256]{1,0:T(8,128)(2,1)} copy(bf16[512,256]{1,0:T(8,128)(2,1)S(1)} %shard_map.64) | data formatting | bytes 524288

commit v7 on v6

--- a/solution.py
+++ b/solution.py
@@ -59,6 +59,7 @@
         return lax.rem(me + i, n)
 
     later = zs - 1 - z
+    early = 1 + n // 2 * (later // (zs - 1))
 
     def at_row(i, plane):
         return lax.rem(y + i, ys) * zs + plane
@@ -189,6 +190,7 @@
     up.start()
     down.start()
     lax.fori_loop(1, n, started(at_copy), 0)
+    lax.fori_loop(1, early, started(ce_copy), 0)
 
     holder = (target // cells).astype(F32)
     s_low = jnp.min(jnp.where(is_local, 1e6, holder), axis=1, keepdims=True)
@@ -231,7 +233,7 @@
     fwd[...] = mine
     picked[rows(me), :] = mine
     lax.fori_loop(1, n, started(fw_copy), 0)
-    lax.fori_loop(1, n, started(ce_copy), 0)
+    lax.fori_loop(early, n, started(ce_copy), 0)
 
     cells_buf[rows(me), :] = ens_ref[:, pl.ds(cell_start(me), 4 * half)]
 

time: 39.1 us -> 38.5 us (0.985)
  Pallas kernels: 37.6 us -> 37 us
    pallas_call x1, Pallas kernels: 37.6 us -> 37 us  [per_device(): pl.pallas_call(kernel, out_shape=jax.ShapeDtypeStruct((cells // n, member...]
where the time goes in v7:
time: 38.5 us; the launch traced here: 38.3 us
  Pallas kernels  37 us (96%)
  local copies, waits for them, and re-layouts  0.71 us (2%)
  between operations  0.66 us (2%)
    pallas_call x1, Pallas kernels, per_device(): pl.pallas_call(kernel, out_shape=jax.ShapeDtypeStruct((cells // n, member...  37 us

profile of v7, /device:TPU:1, one launch (start us, length us, event | category | flops | bytes accessed | tf_op | source)
XLA Modules:
  0.0 38.3 jit_solution(4387127690547618302)
XLA Ops:
  0.7 37.0 %shard_map.64 = bf16[512,256]{1,0:T(8,128)(2,1)S(1)} custom-call(s32[1]{0:T(128)S(6)} %copy.8.count_hbm, bf16[16,8192]{1,0:T(8,128)(2,1)} %ens_hbm.1, f32[1,1024]{1,0:T(1,128)} %rep_hbm.1, s32[1,1024]{1,0:T(1,128)} %cell_hbm.1, f32[4,1024]{1,0:T(4,128)} %bitcast.1, f32[4,512]{1,0:T(4,128)} %bl_hbm.1), custom_call_target="tpu_custom_call" | custom-call | tf_op jit(solution)/shard_map/pallas_call | solution.py:450
  37.6 0.7 %copy.9 = bf16[512,256]{1,0:T(8,128)(2,1)} copy(bf16[512,256]{1,0:T(8,128)(2,1)S(1)} %shard_map.64) | data formatting | bytes 524288
